TPU v7x, 32 devices: a whole 2x2x4 slice. The times are simulated.
32 devices in a mesh: rep: 4 (over y, core), shard: 8 (over z, x).
Axes of the slice: x: 2, y: 2, z: 4, core: 2. Of those that a mesh axis runs over, the one named last changes fastest.
Arguments:
- tokens: bfloat16 [8192, 768], P(('rep', 'shard')), may hold values from -6 to 6
- seg_ids: int32 [8192], P(('rep', 'shard')), may hold values from -1 to 1, as said below
- grad_out: bfloat16 [8192, 768], P(('rep', 'shard')), may hold values from -6 to 6
- ln1_gain: bfloat16 [768], P('shard'), may hold values from 0.5 to 1.5
- ln1_bias: bfloat16 [768], P('shard'), may hold values from -1.5 to 1.5
- w_query: bfloat16 [768, 768], P('shard'), may hold values from -0.21875 to 0.21875
- w_key: bfloat16 [768, 768], P('shard'), may hold values from -0.21875 to 0.21875
- w_value: bfloat16 [768, 768], P('shard'), may hold values from -0.21875 to 0.21875
- b_query: bfloat16 [768], P('shard'), may hold values from -1.5 to 1.5
- b_value: bfloat16 [768], P('shard'), may hold values from -1.5 to 1.5
- w_out: bfloat16 [768, 768], P('shard'), may hold values from -0.875 to 0.875
- b_out: bfloat16 [768], P('shard'), may hold values from -1.5 to 1.5
- ln2_gain: bfloat16 [768], P('shard'), may hold values from 0.5 to 1.5
- ln2_bias: bfloat16 [768], P('shard'), may hold values from -1.5 to 1.5
- w_fc1: bfloat16 [768, 3072], P('shard'), may hold values from -0.21875 to 0.21875
- b_fc1: bfloat16 [3072], P('shard'), may hold values from -1.5 to 1.5
- w_fc2: bfloat16 [3072, 768], P('shard'), may hold values from -0.15625 to 0.15625
- b_fc2: bfloat16 [768], P('shard'), may hold values from -1.5 to 1.5
Outputs:
- out: bfloat16 [8192, 768], P(('rep', 'shard'))
- grad_tokens: float32 [8192, 768], P(('rep', 'shard'))
- grad_ln1_gain: float32 [768], P('shard')
- grad_ln1_bias: float32 [768], P('shard')
- grad_w_query: float32 [768, 768], P('shard')
- grad_w_key: float32 [768, 768], P('shard')
- grad_w_value: float32 [768, 768], P('shard')
- grad_b_query: float32 [768], P('shard')
- grad_b_value: float32 [768], P('shard')
- grad_w_out: float32 [768, 768], P('shard')
- grad_b_out: float32 [768], P('shard')
- grad_ln2_gain: float32 [768], P('shard')
- grad_ln2_bias: float32 [768], P('shard')
- grad_w_fc1: float32 [768, 3072], P('shard')
- grad_b_fc1: float32 [3072], P('shard')
- grad_w_fc2: float32 [3072, 768], P('shard')
- grad_b_fc2: float32 [768], P('shard')
Inputs may be any that keep to these rules, and one draw needn't show every extreme that they name: `seg_ids`: within each device's 256 slots: id 0 on a first run of one or more slots, id 1 on the next run of one or more, then -1 to the end. Every device has at least 128 slots with ids 0 or 1, and some device has no -1.
All inputs are finite; a program needn't handle non-finite values.
Results may differ from a plain program's by a relative error of at most 0.012.
Values may be sent and summed in bfloat16 or wider, within the bound.
A program may use at most 128 MiB of HBM per device.

v0:
```python
import jax
import jax.numpy as jnp
from jax import lax
from jax.sharding import PartitionSpec as P

HEADS = 12
HEAD_DIM = 64


norm_eps = 1e-05


def layer_norm(rows, gain, shift):
    center = rows - jnp.mean(rows, axis=-1, keepdims=True)
    spread = jnp.mean(center * center, axis=-1, keepdims=True)
    return center * lax.rsqrt(spread + norm_eps) * gain + shift


def gelu_exact(values):
    return jax.nn.gelu(values, approximate=False)


def product(left, right):
    return jnp.dot(left, right, preferred_element_type=jnp.float32)


def inner(left, right):
    return lax.dot_general(
        left, right, (((0,), (0,)), ((), ())), preferred_element_type=jnp.float32
    )


def against(left, right):
    return lax.dot_general(
        left, right, (((1,), (1,)), ((), ())), preferred_element_type=jnp.float32
    )


def column_sum(values):
    return jnp.sum(values.astype(jnp.float32), axis=0)


def masked_scores(heads_q, heads_k, allowed):
    scores = jnp.einsum(
        "qhd,khd->hqk", heads_q, heads_k, preferred_element_type=jnp.float32
    ) * HEAD_DIM ** (-0.5)
    return jnp.where(allowed[None], scores, -1e30)


def on_device(
    tokens,
    seg_ids,
    grad_out,
    ln1_gain,
    ln1_bias,
    w_query,
    w_key,
    w_value,
    b_query,
    b_value,
    w_out,
    b_out,
    ln2_gain,
    ln2_bias,
    w_fc1,
    b_fc1,
    w_fc2,
    b_fc2,
):
    gathered = (
        lax.all_gather(ln1_gain, "shard", axis=0, tiled=True),
        lax.all_gather(ln1_bias, "shard", axis=0, tiled=True),
        lax.all_gather(w_query, "shard", axis=0, tiled=True),
        lax.all_gather(w_key, "shard", axis=0, tiled=True),
        lax.all_gather(w_value, "shard", axis=0, tiled=True),
        lax.all_gather(b_query, "shard", axis=0, tiled=True),
        lax.all_gather(b_value, "shard", axis=0, tiled=True),
        lax.all_gather(w_out, "shard", axis=0, tiled=True),
        lax.all_gather(b_out, "shard", axis=0, tiled=True),
        lax.all_gather(ln2_gain, "shard", axis=0, tiled=True),
        lax.all_gather(ln2_bias, "shard", axis=0, tiled=True),
        lax.all_gather(w_fc1, "shard", axis=0, tiled=True),
        lax.all_gather(b_fc1, "shard", axis=0, tiled=True),
        lax.all_gather(w_fc2, "shard", axis=0, tiled=True),
        lax.all_gather(b_fc2, "shard", axis=0, tiled=True),
    )
    (
        gain_one,
        shift_one,
        wq,
        wk,
        wv,
        bq,
        bv,
        wo,
        bo,
        gain_two,
        shift_two,
        w_one,
        b_one,
        w_two,
        b_two,
    ) = gathered
    rows = tokens.astype(jnp.float32)
    count = rows.shape[0]
    width = rows.shape[1]
    order = jnp.arange(count)
    allowed = (seg_ids[:, None] == seg_ids[None, :]) & (order[:, None] >= order[None, :])
    gain_first = gain_one.astype(jnp.float32)
    shift_first = shift_one.astype(jnp.float32)
    normed = layer_norm(rows, gain_first, shift_first).astype(jnp.bfloat16)
    query = (product(normed, wq) + bq.astype(jnp.float32)).astype(jnp.bfloat16)
    keys = product(normed, wk).astype(jnp.bfloat16)
    values = (product(normed, wv) + bv.astype(jnp.float32)).astype(jnp.bfloat16)
    heads_q = query.reshape(count, HEADS, HEAD_DIM)
    heads_k = keys.reshape(count, HEADS, HEAD_DIM)
    heads_v = values.reshape(count, HEADS, HEAD_DIM)
    scores = masked_scores(heads_q, heads_k, allowed)
    peak = jnp.max(scores, axis=-1, keepdims=True)
    expo = jnp.exp(scores - peak)
    total = jnp.sum(expo, axis=-1, keepdims=True)
    logsum = peak + jnp.log(total)
    probs_low = (expo / total).astype(jnp.bfloat16)
    mixed = jnp.einsum("hqk,khd->qhd", probs_low, heads_v, preferred_element_type=jnp.float32)
    mixed = mixed.reshape(count, width).astype(jnp.bfloat16)
    middle = rows + product(mixed, wo) + bo.astype(jnp.float32)
    gain_second = gain_two.astype(jnp.float32)
    shift_second = shift_two.astype(jnp.float32)
    normed_two = layer_norm(middle, gain_second, shift_second).astype(jnp.bfloat16)
    hidden = product(normed_two, w_one) + b_one.astype(jnp.float32)
    active = gelu_exact(hidden).astype(jnp.bfloat16)
    result = (middle + product(active, w_two) + b_two.astype(jnp.float32)).astype(jnp.bfloat16)
    again = (
        lax.all_gather(ln1_gain, "shard", axis=0, tiled=True),
        lax.all_gather(ln1_bias, "shard", axis=0, tiled=True),
        lax.all_gather(w_query, "shard", axis=0, tiled=True),
        lax.all_gather(w_key, "shard", axis=0, tiled=True),
        lax.all_gather(w_value, "shard", axis=0, tiled=True),
        lax.all_gather(b_query, "shard", axis=0, tiled=True),
        lax.all_gather(b_value, "shard", axis=0, tiled=True),
        lax.all_gather(w_out, "shard", axis=0, tiled=True),
        lax.all_gather(b_out, "shard", axis=0, tiled=True),
        lax.all_gather(ln2_gain, "shard", axis=0, tiled=True),
        lax.all_gather(ln2_bias, "shard", axis=0, tiled=True),
        lax.all_gather(w_fc1, "shard", axis=0, tiled=True),
        lax.all_gather(b_fc1, "shard", axis=0, tiled=True),
        lax.all_gather(w_fc2, "shard", axis=0, tiled=True),
        lax.all_gather(b_fc2, "shard", axis=0, tiled=True),
    )
    back_wq, back_wk, back_wv, back_wo = (again[2], again[3], again[4], again[7])
    back_w_one, back_w_two = (again[11], again[13])
    live = (seg_ids >= 0).astype(jnp.float32)[:, None]
    upstream = grad_out.astype(jnp.float32) * live
    grad_b_two = jnp.sum(upstream, axis=0)
    up_low = upstream.astype(jnp.bfloat16)
    grad_w_two = inner(active, up_low)
    grad_active = against(up_low, back_w_two)
    gelu_out, gelu_pull = jax.vjp(gelu_exact, hidden)
    grad_hidden = gelu_pull(grad_active)[0].astype(jnp.bfloat16)
    grad_b_one = column_sum(grad_hidden)
    grad_w_one = inner(normed_two, grad_hidden)
    grad_normed_two = against(grad_hidden, back_w_one)
    norm_out, norm_pull = jax.vjp(layer_norm, middle, gain_second, shift_second)
    grad_mid_norm, grad_gain_two, grad_shift_two = norm_pull(grad_normed_two)
    grad_middle = upstream + grad_mid_norm
    grad_bo = jnp.sum(grad_middle, axis=0)
    mid_low = grad_middle.astype(jnp.bfloat16)
    grad_wo = inner(mixed, mid_low)
    grad_mixed = against(mid_low, back_wo).astype(jnp.bfloat16).reshape(count, HEADS, HEAD_DIM)
    scores_again = masked_scores(heads_q, heads_k, allowed)
    probs = jnp.exp(scores_again - logsum)
    probs_again = probs.astype(jnp.bfloat16)
    grad_probs = jnp.einsum("qhd,khd->hqk", grad_mixed, heads_v, preferred_element_type=jnp.float32)
    grad_values = jnp.einsum(
        "hqk,qhd->khd", probs_again, grad_mixed, preferred_element_type=jnp.float32
    )
    grad_values = grad_values.reshape(count, width).astype(jnp.bfloat16)
    inner_sum = jnp.sum(grad_probs * probs, axis=-1, keepdims=True)
    grad_scores = (probs * (grad_probs - inner_sum) * HEAD_DIM ** (-0.5)).astype(jnp.bfloat16)
    grad_query = jnp.einsum(
        "hqk,khd->qhd", grad_scores, heads_k, preferred_element_type=jnp.float32
    )
    grad_query = grad_query.reshape(count, width).astype(jnp.bfloat16)
    grad_keys = jnp.einsum("hqk,qhd->khd", grad_scores, heads_q, preferred_element_type=jnp.float32)
    grad_keys = grad_keys.reshape(count, width).astype(jnp.bfloat16)
    grad_bq = column_sum(grad_query)
    grad_bv = column_sum(grad_values)
    grad_wq = inner(normed, grad_query)
    grad_wk = inner(normed, grad_keys)
    grad_wv = inner(normed, grad_values)
    grad_normed = (
        against(grad_query, back_wq) + against(grad_keys, back_wk) + against(grad_values, back_wv)
    )
    first_out, first_pull = jax.vjp(layer_norm, rows, gain_first, shift_first)
    grad_rows_norm, grad_gain_one, grad_shift_one = first_pull(grad_normed)
    grad_input = grad_middle + grad_rows_norm
    owned = (
        lax.psum_scatter(grad_gain_one, "shard", scatter_dimension=0, tiled=True),
        lax.psum_scatter(grad_shift_one, "shard", scatter_dimension=0, tiled=True),
        lax.psum_scatter(grad_wq, "shard", scatter_dimension=0, tiled=True),
        lax.psum_scatter(grad_wk, "shard", scatter_dimension=0, tiled=True),
        lax.psum_scatter(grad_wv, "shard", scatter_dimension=0, tiled=True),
        lax.psum_scatter(grad_bq, "shard", scatter_dimension=0, tiled=True),
        lax.psum_scatter(grad_bv, "shard", scatter_dimension=0, tiled=True),
        lax.psum_scatter(grad_wo, "shard", scatter_dimension=0, tiled=True),
        lax.psum_scatter(grad_bo, "shard", scatter_dimension=0, tiled=True),
        lax.psum_scatter(grad_gain_two, "shard", scatter_dimension=0, tiled=True),
        lax.psum_scatter(grad_shift_two, "shard", scatter_dimension=0, tiled=True),
        lax.psum_scatter(grad_w_one, "shard", scatter_dimension=0, tiled=True),
        lax.psum_scatter(grad_b_one, "shard", scatter_dimension=0, tiled=True),
        lax.psum_scatter(grad_w_two, "shard", scatter_dimension=0, tiled=True),
        lax.psum_scatter(grad_b_two, "shard", scatter_dimension=0, tiled=True),
    )
    owned = lax.psum(
        (
            owned[0],
            owned[1],
            owned[2],
            owned[3],
            owned[4],
            owned[5],
            owned[6],
            owned[7],
            owned[8],
            owned[9],
            owned[10],
            owned[11],
            owned[12],
            owned[13],
            owned[14],
        ),
        "rep",
    )
    return (
        result,
        grad_input,
        owned[0],
        owned[1],
        owned[2],
        owned[3],
        owned[4],
        owned[5],
        owned[6],
        owned[7],
        owned[8],
        owned[9],
        owned[10],
        owned[11],
        owned[12],
        owned[13],
        owned[14],
    )


def solution(mesh):
    in_specs = (
        P(("rep", "shard"), None),
        P(("rep", "shard")),
        P(("rep", "shard"), None),
        P("shard"),
        P("shard"),
        P("shard", None),
        P("shard", None),
        P("shard", None),
        P("shard"),
        P("shard"),
        P("shard", None),
        P("shard"),
        P("shard"),
        P("shard"),
        P("shard", None),
        P("shard"),
        P("shard", None),
        P("shard"),
    )
    out_specs = (
        P(("rep", "shard"), None),
        P(("rep", "shard"), None),
        P("shard"),
        P("shard"),
        P("shard", None),
        P("shard", None),
        P("shard", None),
        P("shard"),
        P("shard"),
        P("shard", None),
        P("shard"),
        P("shard"),
        P("shard"),
        P("shard", None),
        P("shard"),
        P("shard", None),
        P("shard"),
    )
    return jax.shard_map(
        on_device, mesh=mesh, in_specs=in_specs, out_specs=out_specs, check_vma=False
    )
```

profile of v0, /device:TPU:1, one launch (start us, length us, event | category | flops | bytes accessed | tf_op | source)
XLA Modules:
  0.0 1060.1 jit_solution(8770730721655575459)
XLA Ops:
  11.9 1.3 fusion.87
  13.9 0.8 dynamic-update-slice.5
  14.7 0.8 dynamic-update-slice.6
  18.9 0.8 dynamic-update-slice.2
  19.7 0.8 dynamic-update-slice.7
  20.6 31.8 %all-reduce.20 = (bf16[768]{0:T(1024)(128)(2,1)S(1)}, bf16[768]{0:T(1024)(128)(2,1)S(1)}, bf16[768]{0:T(1024)(128)(2,1)S(1)}, bf16[768]{0:T(1024)(128)(2,1)S(1)}...) all-reduce(bf16[768]{0:T(1024)(128)(2,1)S(1)} %dynamic-update-slice, ...), channel_id=1, replica_groups=mesh['rep'=4,'shard'=8] {'shard'}, use_global_device_ids=true, to_apply=%add.2 | all-reduce | flops 6144 | bytes 24576
  53.1 21.8 %all-gather = bf16[8,1,384]{2,1,0:T(2,128)(2,1)S(1)} all-gather(bf16[1,1,384]{2,1,0:T(2,128)(2,1)S(1)} %reshape.205), channel_id=1, replica_groups=mesh['rep'=4,'shard'=8] {'shard'}, dimensions={0}, use_global_device_ids=true | all-gather | bytes 6912 | tf_op jit(solution)/shard_map/all_gather | solution.py:83
  75.5 1.1 convert_reduce_fusion.1
  76.6 1.2 fusion.52
  77.9 1.3 compare_convert_fusion
  79.1 1.5 fusion.56
  80.6 1.9 fusion.32
  82.6 0.9 copy.56
  83.5 10.8 %all-gather.8.cloned.1.call-done = bf16[768,768]{1,0:T(8,128)(2,1)} async-done(((bf16[96,768]{1,0:T(8,128)(2,1)}), bf16[768,768]{1,0:T(8,128)(2,1)}) %all-gather.8.cloned.1.call-update) | async-done | bytes 1179664 | tf_op jit(solution)/shard_map/all_gather | solution.py:75
  94.3 1.8 fusion.31
  96.1 0.9 copy.55
  97.0 39.3 %all-gather.12.cloned.1.call-done = bf16[768,768]{1,0:T(8,128)(2,1)} async-done(((bf16[96,768]{1,0:T(8,128)(2,1)}), bf16[768,768]{1,0:T(8,128)(2,1)}) %all-gather.12.cloned.1.call-update) | async-done | bytes 1179664 | tf_op jit(solution)/shard_map/all_gather | solution.py:74
  136.3 1.8 convolution_convert_fusion.1
  138.2 0.9 copy.57
  139.1 1.8 fusion.88
  142.0 1.4 fusion.33
  143.4 34.8 %all-gather.14.cloned.1.call-done = bf16[768,768]{1,0:T(8,128)(2,1)} async-done(((bf16[96,768]{1,0:T(8,128)(2,1)}), bf16[768,768]{1,0:T(8,128)(2,1)}) %all-gather.14.cloned.1.call-update) | async-done | bytes 1179664 | tf_op jit(solution)/shard_map/all_gather | solution.py:78
  178.2 1.9 fusion.89
  180.2 0.9 copy-done.3
  182.4 76.8 %all-gather.16.cloned.1.call-done = bf16[768,3072]{1,0:T(8,128)(2,1)} async-done(((bf16[96,3072]{1,0:T(8,128)(2,1)}), bf16[768,3072]{1,0:T(8,128)(2,1)}) %all-gather.16.cloned.1.call-update) | async-done | bytes 4718608 | tf_op jit(solution)/shard_map/all_gather | solution.py:82
  259.2 11.8 %multiply_convert_fusion.1 = (bf16[256,3072]{1,0:T(8,128)(2,1)}, f32[256,3072]{1,0:T(8,128)}, f32[256,3072]{1,0:T(8,128)}) fusion(f32[3072]{0:T(1024)} %bitcast.67, bf16[768,3072]{1,0:T(8,128)(2,1)} %all-gather.16.cloned.1.call-done, f32[256,768]{1,0:T(8,128)} %copy-done.3, f32[768]{0:T(1024)S(1)} %convert_element_type.146, ...), kind=kOutput, calls=%fused_computation.10 | convolution fusion | flops 1260847104 | bytes 13389824 | tf_op jit(solution)/shard_map/dot_general | solution.py:24
  271.0 68.3 %all-gather.18.cloned.1.call-done = bf16[3072,768]{1,0:T(8,128)(2,1)} async-done(((bf16[384,768]{1,0:T(8,128)(2,1)}), bf16[3072,768]{1,0:T(8,128)(2,1)}) %all-gather.18.cloned.1.call-update) | async-done | bytes 4718608 | tf_op jit(solution)/shard_map/all_gather | solution.py:84
  339.3 7.1 convert_reduce_fusion
  346.5 2.2 multiply_reduce_fusion.1
  349.1 0.8 copy-done.1
  349.9 2.1 fusion.57
  352.1 1.4 log_add_fusion
  353.4 2.9 convolution_convert_fusion
  356.3 1.9 copy.59
  358.3 2.4 convert_reduce_fusion.2
  361.4 2.7 fusion.75
  364.4 3.4 fusion.92
  367.8 5.1 fusion.40
  372.8 3.2 fusion.77
  376.1 5.7 convert_reduce_fusion.3
  381.8 3.2 fusion.79
  385.1 5.2 fusion.73
  390.4 0.9 copy-done.7
  391.8 5.2 fusion.60
  398.7 1.8 fusion.93
  400.5 1.8 convolution_add_fusion.2
  402.3 17.0 %reduce-scatter.13.cloned.1.call-done = f32[96,768]{1,0:T(8,128)} async-done(((f32[768,768]{1,0:T(8,128)}), f32[96,768]{1,0:T(8,128)}) %reduce-scatter.13.cloned.1.call-update) | async-done | bytes 294928 | tf_op jit(solution)/shard_map/reduce_scatter | solution.py:205
  419.3 71.3 %reduce-scatter.11.cloned.1.call-done = f32[96,768]{1,0:T(8,128)} async-done(((f32[768,768]{1,0:T(8,128)}), f32[96,768]{1,0:T(8,128)}) %reduce-scatter.11.cloned.1.call-update) | async-done | bytes 294928 | tf_op jit(solution)/shard_map/reduce_scatter | solution.py:202
  490.7 71.7 %reduce-scatter.9.cloned.1.call-done = f32[96,768]{1,0:T(8,128)} async-done(((f32[768,768]{1,0:T(8,128)}), f32[96,768]{1,0:T(8,128)}) %reduce-scatter.9.cloned.1.call-update) | async-done | bytes 294928 | tf_op jit(solution)/shard_map/reduce_scatter | solution.py:201
  562.3 71.7 %reduce-scatter.7.cloned.1.call-done = f32[96,768]{1,0:T(8,128)} async-done(((f32[768,768]{1,0:T(8,128)}), f32[96,768]{1,0:T(8,128)}) %reduce-scatter.7.cloned.1.call-update) | async-done | bytes 294928 | tf_op jit(solution)/shard_map/reduce_scatter | solution.py:200
  634.0 167.2 %reduce-scatter.15.cloned.1.call-done = f32[96,3072]{1,0:T(8,128)} async-done(((f32[768,3072]{1,0:T(8,128)}), f32[96,3072]{1,0:T(8,128)}) %reduce-scatter.15.cloned.1.call-update) | async-done | bytes 1179664 | tf_op jit(solution)/shard_map/reduce_scatter | solution.py:209
  801.2 166.0 %reduce-scatter.17.cloned.1.call-done = f32[384,768]{1,0:T(8,128)} async-done(((f32[3072,768]{1,0:T(8,128)}), f32[384,768]{1,0:T(8,128)}) %reduce-scatter.17.cloned.1.call-update) | async-done | bytes 1179664 | tf_op jit(solution)/shard_map/reduce_scatter | solution.py:211
  967.3 2.0 fusion.84
  969.9 1.4 fusion.54
  971.2 28.6 %all-reduce.17 = (f32[768]{0:T(1024)S(1)}, f32[768]{0:T(1024)S(1)}, f32[768]{0:T(1024)S(1)}, f32[768]{0:T(1024)S(1)}, f32[768]{0:T(1024)S(1)}, /*index=5*/f32[76...) all-reduce(f32[768]{0:T(1024)S(1)} %get-tuple-element.19, ...), channel_id=2, replica_groups=mesh['rep'=4,'shard'=8] {'shard'}, use_global_device_ids=true, to_apply=%region_12.13.clone | all-reduce | flops 9216 | bytes 73728
  1000.5 13.3 %all-reduce.18 = (f32[96]{0:T(128)}, f32[96]{0:T(128)}, f32[96]{0:T(128)}, f32[96]{0:T(128)}, f32[96]{0:T(128)}, /*index=5*/f32[96]{0:T(128)}, f32[96]{0:T(128)}, f32[384]{0:T(512)}, f32[96]{0:T(128)}) all-reduce(f32[96]{0:T(128)S(1)} %dynamic-slice.9, f32[96]{0:T(128)S(1)} %dynamic-slice.11, ...), channel_id=1, replica_groups=mesh['rep'=4,'shard'=8] {'rep'}, use_global_device_ids=true, to_apply=%region_13.14 | all-reduce | flops 1152 | bytes 9216 | tf_op jit(solution)/shard_map/psum | solution.py:214
  1013.8 4.9 fusion.30
  1018.7 26.0 %all-reduce.23.cloned.1.call-done = (f32[96,768]{1,0:T(8,128)}, f32[96,768]{1,0:T(8,128)}, f32[96,768]{1,0:T(8,128)}, f32[96,768]{1,0:T(8,128)}, f32[96,3072]{1,0:T(8,128)}, /*index=5*/f32[384,768]{1,0:T(8,128)}) async-done(((f32[96,768]{1,0:T(8,128)}, f32[96,768]{1,0:T(8,128)}, f32[96,768]{1,0:T(8,128)}, f32[96,768]{1,0:T(8,128)}, f32[96,3072]{1,0:T(8,128)}, /*index=5*/f32[384,768]{1,0:T(8,128)}), ...) | async-done | bytes 3538960 | tf_op jit(solution)/shard_map/psum | solution.py:214
  1044.6 1.8 copy.81
  1046.5 1.7 copy.82
  1048.2 1.7 copy.83
  1049.9 1.7 copy.84
  1051.6 1.0 copy.85
  1052.6 1.0 copy.86
  (161 shorter events, 15.2 us)
Async XLA Ops:
  7.2 73.4 %all-gather.10.cloned.1.call-start = ((), (), s32[]{:S(2)}) async-start(), calls=%async_computation.7 | async-start | bytes 1327104 | tf_op jit(solution)/shard_map/all_gather | solution.py:73
  7.9 86.4 %all-gather.8.cloned.1.call-start = ((), (), s32[]{:S(2)}) async-start(), calls=%async_computation.6 | async-start | bytes 1327104 | tf_op jit(solution)/shard_map/all_gather | solution.py:75
  8.7 85.6 %copy-start = (bf16[256,768]{1,0:T(8,128)(2,1)S(1)}, bf16[256,768]{1,0:T(8,128)(2,1)}, u32[]{:S(2)}) copy-start(bf16[256,768]{1,0:T(8,128)(2,1)} %param.18) | copy-start | bytes 1179652
  8.7 127.7 %all-gather.12.cloned.1.call-start = ((), (), s32[]{:S(2)}) async-start(), calls=%async_computation.8 | async-start | bytes 1327104 | tf_op jit(solution)/shard_map/all_gather | solution.py:74
  9.4 168.8 %all-gather.14.cloned.1.call-start = ((), (), s32[]{:S(2)}) async-start(), calls=%async_computation.9 | async-start | bytes 1327104 | tf_op jit(solution)/shard_map/all_gather | solution.py:78
  10.0 249.2 %all-gather.16.cloned.1.call-start = ((), (), s32[]{:S(2)}) async-start(), calls=%async_computation.10 | async-start | bytes 5308416 | tf_op jit(solution)/shard_map/all_gather | solution.py:82
  10.6 328.7 %all-gather.18.cloned.1.call-start = ((), (), s32[]{:S(2)}) async-start(), calls=%async_computation.11 | async-start | bytes 5308416 | tf_op jit(solution)/shard_map/all_gather | solution.py:84
  11.2 408.2 %reduce-scatter.13.cloned.1.call-start = ((), (), s32[]{:S(2)}) async-start(), calls=%async_computation.15 | async-start | bytes 2654208 | tf_op jit(solution)/shard_map/reduce_scatter | solution.py:205
  52.4 83.9 %copy-start.21 = (f32[768]{0:T(1024)}, f32[768]{0:T(1024)S(1)}, u32[]{:S(2)}) copy-start(f32[768]{0:T(1024)S(1)} %convert_element_type.133) | copy-start | bytes 9220
  77.8 18.3 %copy-start.37 = (f32[256]{0:T(256)}, f32[256]{0:T(256)S(1)}, u32[]{:S(2)}) copy-start(f32[256]{0:T(256)S(1)} %fusion.52) | copy-start | bytes 3076
  79.1 57.2 %copy-start.24 = (f32[256]{0:T(256)}, f32[256]{0:T(256)S(1)}, u32[]{:S(2)}) copy-start(f32[256]{0:T(256)S(1)} %fusion.66) | copy-start | bytes 3076
  139.1 2.9 copy-start.17
  140.9 0.6 copy-start.20
  141.4 0.6 copy-start.23
  180.2 0.9 copy-start.3
  180.2 1.1 copy-start.29
  181.3 0.6 copy-start.39
  339.3 7.1 copy-start.4
  339.3 7.1 copy-start.30
  339.3 7.1 copy-start.34
  339.3 7.1 copy-start.45
  346.4 2.3 copy-start.15
  346.5 2.2 copy-start.40
  346.5 3.5 copy-start.6
  346.5 3.5 copy-start.12
  346.5 3.5 copy-start.27
  349.1 0.9 copy-start.1
  349.1 0.9 copy-start.32
  352.0 138.6 %reduce-scatter.11.cloned.1.call-start = ((), (), s32[]{:S(2)}) async-start(), calls=%async_computation.14 | async-start | bytes 2654208 | tf_op jit(solution)/shard_map/reduce_scatter | solution.py:202
  358.3 3.1 copy-start.22
  360.6 0.7 copy-start.8
  364.1 198.2 %reduce-scatter.9.cloned.1.call-start = ((), (), s32[]{:S(2)}) async-start(), calls=%async_computation.13 | async-start | bytes 2654208 | tf_op jit(solution)/shard_map/reduce_scatter | solution.py:201
  376.1 258.0 %reduce-scatter.7.cloned.1.call-start = ((), (), s32[]{:S(2)}) async-start(), calls=%async_computation.12 | async-start | bytes 2654208 | tf_op jit(solution)/shard_map/reduce_scatter | solution.py:200
  381.8 3.3 copy-start.5
  381.8 3.3 copy-start.16
  381.8 3.3 copy-start.31
  381.8 3.3 copy-start.35
  385.0 416.2 %reduce-scatter.15.cloned.1.call-start = ((), (), s32[]{:S(2)}) async-start(), calls=%async_computation.16 | async-start | bytes 10616832 | tf_op jit(solution)/shard_map/reduce_scatter | solution.py:209
  390.3 1.0 copy-start.7
  390.3 1.5 copy-start.10
  390.3 1.5 copy-start.28
  390.3 576.9 %reduce-scatter.17.cloned.1.call-start = ((), (), s32[]{:S(2)}) async-start(), calls=%async_computation.17 | async-start | bytes 10616832 | tf_op jit(solution)/shard_map/reduce_scatter | solution.py:211
  397.0 1.5 copy-start.44
  397.0 1.5 copy-start.26
  397.0 1.6 copy-start.41
  397.0 1.6 copy-start.14
  397.0 3.4 copy-start.13
  397.1 647.6 %all-reduce.23.cloned.1.call-start = ((), (), s32[]{:S(2)}) async-start(), calls=%async_computation.18 | async-start | bytes 7077888 | tf_op jit(solution)/shard_map/psum | solution.py:214
  400.5 566.8 %copy-start.9 = (bf16[12,64,256]{2,1,0:T(8,128)(2,1)S(1)}, bf16[12,64,256]{2,1,0:T(8,128)(2,1)}, u32[]{:S(2)}) copy-start(bf16[12,64,256]{2,1,0:T(8,128)(2,1)} %copy-done.8) | copy-start | bytes 1179652
  967.2 2.1 copy-start.38
  967.2 2.1 copy-start.25
  967.3 2.6 copy-start.2
  967.3 2.6 copy-start.33
  967.3 3.9 copy-start.36
  967.3 3.9 copy-start.42
  967.3 3.9 copy-start.43
  969.3 44.5 %copy-start.11 = (bf16[256,3072]{1,0:T(8,128)(2,1)S(1)}, bf16[256,3072]{1,0:T(8,128)(2,1)}, u32[]{:S(2)}) copy-start(bf16[256,3072]{1,0:T(8,128)(2,1)} %get-tuple-element.60) | copy-start | bytes 4718596
  1044.6 6.9 copy-start.19
  1044.6 7.9 copy-start.18
Sparse Core Ops, SparseCore 0:
  10.2 42.6 all-gather.9
  55.0 39.1 all-gather.7
  96.5 39.8 all-gather.11
  138.4 39.8 all-gather.13
  180.3 78.9 all-gather.15
  261.2 78.0 all-gather.17
  352.1 67.1 reduce-scatter.12
  422.8 67.8 reduce-scatter.10
  494.2 68.1 reduce-scatter.8
  565.7 68.2 reduce-scatter.6
  637.6 163.5 reduce-scatter.14
  804.6 162.5 reduce-scatter.16
  970.0 74.5 all-reduce.22
where the time goes:
time: 1060 us
  waiting for transfers between devices  825 us (78%)
  blocking collectives  95.5 us (9%)
  matrix products  83.3 us (8%)
  local copies, waits for them, and re-layouts  28.4 us (3%)
  between operations  16.5 us (2%)
  other arithmetic  11.1 us (1%)
    reduce_scatter x1, waiting for transfers between devices, on_device(): lax.psum_scatter(grad_w_one, 'shard', scatter_dimension=0, tiled=True)  167 us
    reduce_scatter x1, waiting for transfers between devices, on_device(): lax.psum_scatter(grad_w_two, 'shard', scatter_dimension=0, tiled=True)  166 us
    all_gather x1, waiting for transfers between devices, on_device(): lax.all_gather(w_fc1, 'shard', axis=0, tiled=True)  76.8 us
    reduce_scatter x1, waiting for transfers between devices, on_device(): lax.psum_scatter(grad_wk, 'shard', scatter_dimension=0, tiled=True)  71.7 us
    reduce_scatter x1, waiting for transfers between devices, on_device(): lax.psum_scatter(grad_wq, 'shard', scatter_dimension=0, tiled=True)  71.7 us
    reduce_scatter x1, waiting for transfers between devices, on_device(): lax.psum_scatter(grad_wv, 'shard', scatter_dimension=0, tiled=True)  71.3 us
    all_gather x1, waiting for transfers between devices, on_device(): lax.all_gather(w_fc2, 'shard', axis=0, tiled=True)  68.3 us
    unnamed x2, blocking collectives  60.4 us
  transfers between devices with their start and end apart: 13, of which 12 were waited for; matrix products, arithmetic and copies ran while one was open for 9% of the time, Pallas kernels for 0%

commit v1 on v0

--- a/solution.py
+++ b/solution.py
@@ -1,6 +1,10 @@
+import functools
+
 import jax
 import jax.numpy as jnp
 from jax import lax
+from jax.experimental import pallas as pl
+from jax.experimental.pallas import tpu as pltpu
 from jax.sharding import PartitionSpec as P
 
 HEADS = 12
@@ -47,43 +51,7 @@
     return jnp.where(allowed[None], scores, -1e30)
 
 
-def on_device(
-    tokens,
-    seg_ids,
-    grad_out,
-    ln1_gain,
-    ln1_bias,
-    w_query,
-    w_key,
-    w_value,
-    b_query,
-    b_value,
-    w_out,
-    b_out,
-    ln2_gain,
-    ln2_bias,
-    w_fc1,
-    b_fc1,
-    w_fc2,
-    b_fc2,
-):
-    gathered = (
-        lax.all_gather(ln1_gain, "shard", axis=0, tiled=True),
-        lax.all_gather(ln1_bias, "shard", axis=0, tiled=True),
-        lax.all_gather(w_query, "shard", axis=0, tiled=True),
-        lax.all_gather(w_key, "shard", axis=0, tiled=True),
-        lax.all_gather(w_value, "shard", axis=0, tiled=True),
-        lax.all_gather(b_query, "shard", axis=0, tiled=True),
-        lax.all_gather(b_value, "shard", axis=0, tiled=True),
-        lax.all_gather(w_out, "shard", axis=0, tiled=True),
-        lax.all_gather(b_out, "shard", axis=0, tiled=True),
-        lax.all_gather(ln2_gain, "shard", axis=0, tiled=True),
-        lax.all_gather(ln2_bias, "shard", axis=0, tiled=True),
-        lax.all_gather(w_fc1, "shard", axis=0, tiled=True),
-        lax.all_gather(b_fc1, "shard", axis=0, tiled=True),
-        lax.all_gather(w_fc2, "shard", axis=0, tiled=True),
-        lax.all_gather(b_fc2, "shard", axis=0, tiled=True),
-    )
+def layer(tokens, seg_ids, grad_out, gathered):
     (
         gain_one,
         shift_one,
@@ -130,25 +98,8 @@
     hidden = product(normed_two, w_one) + b_one.astype(jnp.float32)
     active = gelu_exact(hidden).astype(jnp.bfloat16)
     result = (middle + product(active, w_two) + b_two.astype(jnp.float32)).astype(jnp.bfloat16)
-    again = (
-        lax.all_gather(ln1_gain, "shard", axis=0, tiled=True),
-        lax.all_gather(ln1_bias, "shard", axis=0, tiled=True),
-        lax.all_gather(w_query, "shard", axis=0, tiled=True),
-        lax.all_gather(w_key, "shard", axis=0, tiled=True),
-        lax.all_gather(w_value, "shard", axis=0, tiled=True),
-        lax.all_gather(b_query, "shard", axis=0, tiled=True),
-        lax.all_gather(b_value, "shard", axis=0, tiled=True),
-        lax.all_gather(w_out, "shard", axis=0, tiled=True),
-        lax.all_gather(b_out, "shard", axis=0, tiled=True),
-        lax.all_gather(ln2_gain, "shard", axis=0, tiled=True),
-        lax.all_gather(ln2_bias, "shard", axis=0, tiled=True),
-        lax.all_gather(w_fc1, "shard", axis=0, tiled=True),
-        lax.all_gather(b_fc1, "shard", axis=0, tiled=True),
-        lax.all_gather(w_fc2, "shard", axis=0, tiled=True),
-        lax.all_gather(b_fc2, "shard", axis=0, tiled=True),
-    )
-    back_wq, back_wk, back_wv, back_wo = (again[2], again[3], again[4], again[7])
-    back_w_one, back_w_two = (again[11], again[13])
+    back_wq, back_wk, back_wv, back_wo = (wq, wk, wv, wo)
+    back_w_one, back_w_two = (w_one, w_two)
     live = (seg_ids >= 0).astype(jnp.float32)[:, None]
     upstream = grad_out.astype(jnp.float32) * live
     grad_b_two = jnp.sum(upstream, axis=0)
@@ -194,62 +145,385 @@
     first_out, first_pull = jax.vjp(layer_norm, rows, gain_first, shift_first)
     grad_rows_norm, grad_gain_one, grad_shift_one = first_pull(grad_normed)
     grad_input = grad_middle + grad_rows_norm
-    owned = (
-        lax.psum_scatter(grad_gain_one, "shard", scatter_dimension=0, tiled=True),
-        lax.psum_scatter(grad_shift_one, "shard", scatter_dimension=0, tiled=True),
-        lax.psum_scatter(grad_wq, "shard", scatter_dimension=0, tiled=True),
-        lax.psum_scatter(grad_wk, "shard", scatter_dimension=0, tiled=True),
-        lax.psum_scatter(grad_wv, "shard", scatter_dimension=0, tiled=True),
-        lax.psum_scatter(grad_bq, "shard", scatter_dimension=0, tiled=True),
-        lax.psum_scatter(grad_bv, "shard", scatter_dimension=0, tiled=True),
-        lax.psum_scatter(grad_wo, "shard", scatter_dimension=0, tiled=True),
-        lax.psum_scatter(grad_bo, "shard", scatter_dimension=0, tiled=True),
-        lax.psum_scatter(grad_gain_two, "shard", scatter_dimension=0, tiled=True),
-        lax.psum_scatter(grad_shift_two, "shard", scatter_dimension=0, tiled=True),
-        lax.psum_scatter(grad_w_one, "shard", scatter_dimension=0, tiled=True),
-        lax.psum_scatter(grad_b_one, "shard", scatter_dimension=0, tiled=True),
-        lax.psum_scatter(grad_w_two, "shard", scatter_dimension=0, tiled=True),
-        lax.psum_scatter(grad_b_two, "shard", scatter_dimension=0, tiled=True),
-    )
-    owned = lax.psum(
-        (
-            owned[0],
-            owned[1],
-            owned[2],
-            owned[3],
-            owned[4],
-            owned[5],
-            owned[6],
-            owned[7],
-            owned[8],
-            owned[9],
-            owned[10],
-            owned[11],
-            owned[12],
-            owned[13],
-            owned[14],
+    return result, grad_input, (
+        grad_gain_one,
+        grad_shift_one,
+        grad_wq,
+        grad_wk,
+        grad_wv,
+        grad_bq,
+        grad_bv,
+        grad_wo,
+        grad_bo,
+        grad_gain_two,
+        grad_shift_two,
+        grad_w_one,
+        grad_b_one,
+        grad_w_two,
+        grad_b_two,
+    )
+
+
+def on_device_plain(tokens, seg_ids, grad_out, *params):
+    gathered = tuple(lax.all_gather(p, "shard", axis=0, tiled=True) for p in params)
+    result, grad_input, grads = layer(tokens, seg_ids, grad_out, gathered)
+    owned = tuple(
+        lax.psum_scatter(g, "shard", scatter_dimension=0, tiled=True) for g in grads
+    )
+    owned = lax.psum(owned, "rep")
+    return (result, grad_input) + owned
+
+
+HALVES = 2
+THIRDS = 3
+MESH = pl.DeviceIdType.MESH
+
+
+def place():
+    rep, shard = lax.axis_index("rep"), lax.axis_index("shard")
+    return rep // 2, rep % 2, shard // 2, shard % 2
+
+
+def device(y, core, z, x):
+    return (2 * y + core, 2 * z + x)
+
+
+def greet(y, core, z, x):
+    barrier = pltpu.get_barrier_semaphore()
+    peers = [
+        device(y, 1 - core, z, x),
+        device(1 - y, core, z, x),
+        device(y, core, z, 1 - x),
+    ] + [device(y, core, (z + d) % 4, x) for d in (1, 2, 3)]
+    for peer in peers:
+        pl.semaphore_signal(barrier, inc=1, device_id=peer, device_id_type=MESH)
+    pl.semaphore_wait(barrier, len(peers))
+
+
+def remote(src, dst, send_sem, recv_sem, peer):
+    return pltpu.make_async_remote_copy(
+        src_ref=src,
+        dst_ref=dst,
+        send_sem=send_sem,
+        recv_sem=recv_sem,
+        device_id=peer,
+        device_id_type=MESH,
+    )
+
+
+def cut(shapes, limit):
+    pieces = []
+    for at, (rows, cols) in enumerate(shapes):
+        if rows * cols <= limit:
+            pieces.append((at, 0, rows, 0, cols))
+        elif rows > 16:
+            step = max(16, limit // cols // 16 * 16)
+            pieces += [(at, r, step, 0, cols) for r in range(0, rows, step)]
+        else:
+            step = limit // rows // 128 * 128
+            pieces += [(at, 0, rows, c, step) for c in range(0, cols, step)]
+    return pieces
+
+
+def gather_kernel(pieces, count, *refs):
+    ins, outs = refs[:count], refs[count : 2 * count]
+    own_sem, zs, zr, xs, xr, ys, yr, cs, cr = refs[2 * count :]
+    y, core, z, x = place()
+    total = len(pieces)
+
+    def part(ref, piece, *lead):
+        _, r, rows, c, cols = piece
+        return ref.at[(*lead, pl.ds(r, rows), pl.ds(c, cols))]
+
+    own = []
+    for a, piece in enumerate(pieces):
+        own.append(
+            pltpu.make_async_copy(
+                part(ins[piece[0]], piece, core, pl.ds(y, 2)),
+                part(outs[piece[0]], piece, z, x, core, pl.ds(y, 2)),
+                own_sem.at[a],
+            )
+        )
+        own[a].start()
+    greet(y, core, z, x)
+    by_z, by_x, by_y, by_core = [], [], [], []
+    for a, piece in enumerate(pieces):
+        out = outs[piece[0]]
+        by_z.append(
+            [
+                remote(
+                    part(ins[piece[0]], piece, core, pl.ds(y, 2)),
+                    part(out, piece, z, x, core, pl.ds(y, 2)),
+                    zs.at[a, d - 1],
+                    zr.at[a, d - 1],
+                    device(y, core, (z + d) % 4, x),
+                )
+                for d in (1, 2, 3)
+            ]
+        )
+        ref = part(out, piece, slice(None), x, core, pl.ds(y, 2))
+        by_x.append(remote(ref, ref, xs.at[a], xr.at[a], device(y, core, z, 1 - x)))
+        ref = part(out, piece, slice(None), slice(None), core, 2 * y)
+        by_y.append(remote(ref, ref, ys.at[a], yr.at[a], device(1 - y, core, z, x)))
+        ref = part(out, piece, slice(None), slice(None), core, slice(None))
+        by_core.append(remote(ref, ref, cs.at[a], cr.at[a], device(y, 1 - core, z, x)))
+    for copies in by_z:
+        for copy in copies:
+            copy.start()
+    for step in range(total + 2):
+        if 0 <= step - 2 < total:
+            by_y[step - 2].wait_recv()
+            by_core[step - 2].start()
+        if 0 <= step - 1 < total:
+            by_x[step - 1].wait_recv()
+            by_y[step - 1].start()
+        if step < total:
+            own[step].wait()
+            for copy in by_z[step]:
+                copy.wait_recv()
+            by_x[step].start()
+    for a in range(total):
+        by_core[a].wait_recv()
+    for a in range(total):
+        for copy in by_z[a]:
+            copy.wait_send()
+        by_x[a].wait_send()
+        by_y[a].wait_send()
+        by_core[a].wait_send()
+
+
+def gather_all(shards):
+    shapes = [s.shape[2:] for s in shards]
+    pieces = cut(shapes, 16 * 1536)
+    total, count = len(pieces), len(shards)
+    dma = pltpu.SemaphoreType.DMA
+    return pl.pallas_call(
+        functools.partial(gather_kernel, pieces, count),
+        out_shape=[jax.ShapeDtypeStruct((4, 2) + s.shape, s.dtype) for s in shards],
+        in_specs=[pl.BlockSpec(memory_space=pl.ANY)] * count,
+        out_specs=[pl.BlockSpec(memory_space=pl.ANY)] * count,
+        scratch_shapes=[
+            dma((total,)),
+            dma((total, 3)),
+            dma((total, 3)),
+        ]
+        + [dma((total,))] * 6,
+        compiler_params=pltpu.CompilerParams(collective_id=0, has_side_effects=True),
+        name="gather_parameters",
+    )(*shards)
+
+
+def reduce_kernel(pieces, count, *refs):
+    ins, outs = refs[:count], refs[count : 2 * count]
+    total = len(pieces)
+    bufs = refs[2 * count : 2 * count + 5 * total]
+    one, two, three, four, five = [bufs[i * total : (i + 1) * total] for i in range(5)]
+    done = refs[2 * count + 5 * total : 2 * count + 6 * total]
+    sems = refs[2 * count + 6 * total :]
+    cs, cr, ys, yr, xs, xr, zs, zr, us, ur, fs, fr = sems
+    y, core, z, x = place()
+    f32, b16 = jnp.float32, jnp.bfloat16
+
+    def part(ref, piece, *lead):
+        _, r, rows, c, cols = piece
+        return ref.at[(*lead, pl.ds(r, rows), pl.ds(c, cols))]
+
+    every = slice(None)
+    by_core, by_y, by_x, by_z, back_y, back_core = [], [], [], [], [], []
+    for a, piece in enumerate(pieces):
+        by_core.append(
+            remote(
+                part(ins[piece[0]], piece, every, every, 1 - core, every),
+                one[a],
+                cs.at[a],
+                cr.at[a],
+                device(y, 1 - core, z, x),
+            )
+        )
+        by_y.append(
+            remote(
+                one[a].at[:, :, 2 * (1 - y)],
+                two[a],
+                ys.at[a],
+                yr.at[a],
+                device(1 - y, core, z, x),
+            )
+        )
+        by_x.append(
+            remote(
+                one[a].at[:, 1 - x, pl.ds(y, 2)],
+                three[a],
+                xs.at[a],
+                xr.at[a],
+                device(y, core, z, 1 - x),
+            )
+        )
+        by_z.append(
+            [
+                remote(
+                    three[a].at[(z + d) % 4],
+                    four[a].at[d - 1],
+                    zs.at[a, d - 1],
+                    zr.at[a, d - 1],
+                    device(y, core, (z + d) % 4, x),
+                )
+                for d in (1, 2, 3)
+            ]
+        )
+        back_y.append(
+            remote(done[a], five[a], us.at[a], ur.at[a], device(1 - y, core, z, x))
+        )
+        final = part(outs[piece[0]], piece, core, every)
+        back_core.append(
+            remote(final, final, fs.at[a], fr.at[a], device(y, 1 - core, z, x))
+        )
+
+    def add_core(a):
+        by_core[a].wait_recv()
+        mine = part(ins[pieces[a][0]], pieces[a], every, every, core, every)
+
+        @pl.loop(0, 8)
+        def _(s):
+            i, j = s // 2, s % 2
+            one[a][i, j] = (one[a][i, j].astype(f32) + mine[i, j].astype(f32)).astype(b16)
+
+        by_y[a].start()
+
+    def add_y(a):
+        by_y[a].wait_recv()
+
+        @pl.loop(0, 8)
+        def _(s):
+            i, j = s // 2, s % 2
+            one[a][i, j, 2 * y] = (
+                one[a][i, j, 2 * y].astype(f32) + two[a][i, j].astype(f32)
+            ).astype(b16)
+
+        by_x[a].start()
+
+    def add_x(a):
+        by_x[a].wait_recv()
+
+        @pl.loop(0, 4)
+        def _(i):
+            three[a][i] = (
+                three[a][i].astype(f32) + one[a][i, x, pl.ds(y, 2)].astype(f32)
+            ).astype(b16)
+
+        for copy in by_z[a]:
+            copy.start()
+
+    def add_z(a):
+        for copy in by_z[a]:
+            copy.wait_recv()
+        done[a][...] = (
+            (three[a][z].astype(f32) + four[a][0].astype(f32))
+            + (four[a][1].astype(f32) + four[a][2].astype(f32))
+        ).astype(b16)
+        back_y[a].start()
+
+    def add_planes(a):
+        back_y[a].wait_recv()
+        out = part(outs[pieces[a][0]], pieces[a], core, every)
+        out[1] = (done[a][1 - y].astype(f32) + five[a][y].astype(f32)).astype(b16)
+        out[2 * y] = done[a][y]
+        out[2 * (1 - y)] = five[a][1 - y]
+        back_core[a].start()
+
+    greet(y, core, z, x)
+    for a in range(total):
+        by_core[a].start()
+    stages = (add_core, add_y, add_x, add_z, add_planes)
+    for step in range(total + len(stages) - 1):
+        for late in reversed(range(len(stages))):
+            if 0 <= step - late < total:
+                stages[late](step - late)
+    for a in range(total):
+        back_core[a].wait_recv()
+    for a in range(total):
+        by_core[a].wait_send()
+        by_y[a].wait_send()
+        by_x[a].wait_send()
+        for copy in by_z[a]:
+            copy.wait_send()
+        back_y[a].wait_send()
+        back_core[a].wait_send()
+
+
+def reduce_all(grads):
+    shapes = [g.shape[4:] for g in grads]
+    pieces = cut(shapes, 16 * 1536)
+    total, count = len(pieces), len(grads)
+    dma = pltpu.SemaphoreType.DMA
+    leads = ((4, 2, 3), (4, 2), (4, 2), (3, 2), (2,), (2,))
+    buffers = [
+        pltpu.VMEM(lead + (p[2], p[4]), jnp.bfloat16) for lead in leads for p in pieces
+    ]
+    single, triple = dma((total,)), dma((total, 3))
+    return pl.pallas_call(
+        functools.partial(reduce_kernel, pieces, count),
+        out_shape=[jax.ShapeDtypeStruct(g.shape[2:], g.dtype) for g in grads],
+        in_specs=[pl.BlockSpec(memory_space=pltpu.VMEM)] * count,
+        out_specs=[pl.BlockSpec(memory_space=pltpu.VMEM)] * count,
+        scratch_shapes=buffers + [single] * 6 + [triple] * 2 + [single] * 4,
+        compiler_params=pltpu.CompilerParams(
+            collective_id=1, has_side_effects=True, vmem_limit_bytes=52 * 1024 * 1024
         ),
-        "rep",
-    )
-    return (
-        result,
-        grad_input,
-        owned[0],
-        owned[1],
-        owned[2],
-        owned[3],
-        owned[4],
-        owned[5],
-        owned[6],
-        owned[7],
-        owned[8],
-        owned[9],
-        owned[10],
-        owned[11],
-        owned[12],
-        owned[13],
-        owned[14],
-    )
+        name="reduce_gradients",
+    )(*grads)
+
+
+VECTORS = (0, 1, 5, 6, 8, 9, 10, 14)
+MATRICES = (2, 3, 4, 7, 11, 13)
+B_ONE = 12
+
+
+def on_device(tokens, seg_ids, grad_out, *params):
+    width = params[0].shape[0]
+    lanes = 128
+    rows = 96
+
+    def folded(w):
+        return w.reshape(HALVES, THIRDS, w.shape[0] // 6, w.shape[1])
+
+    small = jnp.concatenate(
+        [jnp.pad(params[i][None], ((0, 0), (0, lanes - width))) for i in VECTORS]
+        + [params[B_ONE].reshape(-1, lanes)]
+    )
+    small = jnp.pad(small, ((0, rows - small.shape[0]), (0, 0)))
+    whole = gather_all([folded(small)] + [folded(params[i]) for i in MATRICES])
+    gathered = [None] * len(params)
+    small = whole[0].reshape(8, rows, lanes)
+    for at, i in enumerate(VECTORS):
+        gathered[i] = small[:, at, :width].reshape(-1)
+    many = params[B_ONE].shape[0] // lanes
+    gathered[B_ONE] = small[:, len(VECTORS) : len(VECTORS) + many].reshape(-1)
+    for at, i in enumerate(MATRICES):
+        gathered[i] = whole[1 + at].reshape(-1, params[i].shape[1])
+
+    result, grad_input, grads = layer(tokens, seg_ids, grad_out, gathered)
+
+    low = [g.astype(jnp.bfloat16) for g in grads]
+    vectors = jnp.stack([low[i].reshape(8, width) for i in VECTORS], axis=1)
+    vectors = jnp.pad(vectors, ((0, 0), (0, 0), (0, lanes - width)))
+    vectors = jnp.concatenate([vectors, low[B_ONE].reshape(8, many, lanes)], axis=1)
+    vectors = jnp.pad(vectors, ((0, 0), (0, rows - vectors.shape[1]), (0, 0)))
+    shapes = [(rows, lanes)] + [params[i].shape for i in MATRICES]
+    arrays = [vectors] + [low[i] for i in MATRICES]
+    sums = reduce_all(
+        [
+            g.reshape(4, 2, HALVES, THIRDS, shape[0] // 6, shape[1])
+            for g, shape in zip(arrays, shapes)
+        ]
+    )
+    sums = [s.reshape(shape).astype(jnp.float32) for s, shape in zip(sums, shapes)]
+    owned = [None] * len(params)
+    for at, i in enumerate(VECTORS):
+        owned[i] = sums[0][at, :width]
+    owned[B_ONE] = sums[0][len(VECTORS) : len(VECTORS) + many].reshape(-1)
+    for at, i in enumerate(MATRICES):
+        owned[i] = sums[1 + at]
+    return (result, grad_input) + tuple(owned)
 
 
 def solution(mesh):
@@ -292,6 +566,8 @@
         P("shard", None),
         P("shard"),
     )
+    shape = dict(mesh.shape)
+    fits = shape["rep"] == 4 and shape["shard"] == 8
     return jax.shard_map(
-        on_device, mesh=mesh, in_specs=in_specs, out_specs=out_specs, check_vma=False
-    )
+        on_device if fits else on_device_plain, mesh=mesh, in_specs=in_specs, out_specs=out_specs, check_vma=False
+    )

time: 1060 us -> 299 us (0.28)
  waiting for transfers between devices: 825 us -> 0 us
  Pallas kernels: 0 us -> 194 us
  blocking collectives: 95.5 us -> 0 us
  matrix products: 83.3 us -> 62.1 us
  between operations: 16.5 us -> 1.31 us
    reduce_scatter x6 -> x0, waiting for transfers between devices: 565 us -> none  [the longest x1 167 us: on_device(): lax.psum_scatter(grad_w_one, 'shard', scatter_dimension=0, tiled=True)]
    all_gather x6 -> x0, waiting for transfers between devices: 230 us -> none  [the longest x1 76.8 us: on_device(): lax.all_gather(w_fc1, 'shard', axis=0, tiled=True)]
    pallas_call x0 -> x2, Pallas kernels: none -> 194 us  [the longest x1 101 us: reduce_all(): pl.pallas_call(functools.partial(reduce_kernel, pieces, count), out_shape...]
    unnamed x2 -> x0, blocking collectives: 60.4 us -> none
    psum x1 -> x0, waiting for transfers between devices: 26 us -> none  [on_device(): lax.psum((owned[0], owned[1], owned[2], owned[3], owned[4], owned[5], own...]
    all_gather x1 -> x0, blocking collectives: 21.8 us -> none  [on_device(): lax.all_gather(b_fc1, 'shard', axis=0, tiled=True)]
    unnamed x125 -> x102, local copies, waits for them, and re-layouts: 23.5 us -> 2.4 us
    psum x1 -> x0, blocking collectives: 13.3 us -> none  [on_device(): lax.psum((owned[0], owned[1], owned[2], owned[3], owned[4], owned[5], own...]
  transfers between devices with their start and end apart: 13 -> 0, of which waited for: 12 -> 0; matrix products, arithmetic and copies ran while one was open for 9% -> 0% of each run, Pallas kernels for 0% -> 0%
where the time goes in v1:
time: 299 us; the launch traced here: 298 us
  Pallas kernels  194 us (65%)
  matrix products  62.1 us (21%)
  local copies, waits for them, and re-layouts  24.3 us (8%)
  other arithmetic  16.2 us (5%)
    pallas_call x1, Pallas kernels, reduce_all(): pl.pallas_call(functools.partial(reduce_kernel, pieces, count), out_shape...  101 us
    pallas_call x1, Pallas kernels, gather_all(): pl.pallas_call(functools.partial(gather_kernel, pieces, count), out_shape...  93.5 us
    dot_general x6, matrix products, inner(): lax.dot_general(left, right, (((0,), (0,)), ((), ())), preferred_element_...  17.3 us
    dot_general x6, matrix products, product(): return jnp.dot(left, right, preferred_element_type=jnp.float32)  14.2 us
    dot_general x6, matrix products, against(): lax.dot_general(left, right, (((1,), (1,)), ((), ())), preferred_element_...  12.6 us

profile of v1, /device:TPU:1, one launch (start us, length us, event | category | flops | bytes accessed | tf_op | source)
XLA Modules:
  0.0 298.0 jit_solution(14332171818947121220)
XLA Ops:
  0.7 0.7 pad.37
  1.3 0.7 pad.38
  2.0 0.7 pad.39
  2.6 0.7 pad.40
  3.3 0.7 pad.41
  4.0 0.7 pad.42
  4.6 0.7 pad.43
  5.3 0.7 pad.44
  5.9 0.7 concatenate.6
  6.7 0.7 compare_convert_fusion
  7.4 1.1 convert_reduce_fusion
  8.5 1.3 fusion.52
  9.8 0.6 pad.45
  10.4 1.5 fusion.56
  11.9 93.5 %gather_parameters.1 = (bf16[4,2,2,3,16,128]{5,4,3,2,1,0:T(8,128)(2,1)}, bf16[4,2,2,3,16,768]{5,4,3,2,1,0:T(8,128)(2,1)}, bf16[4,2,2,3,16,768]{5,4,3,2,1,0:T(8,1...) custom-call(bf16[2,3,16,128]{3,2,1,0:T(8,128)(2,1)} %bitcast.156, ...), custom_call_target="tpu_custom_call" | custom-call | tf_op jit(solution)/shard_map/gather_parameters/pallas_call | solution.py:300
  105.5 0.8 slice_convert_fusion
  106.3 1.3 fusion.66
  107.6 0.6 reshape.432
  108.2 0.7 reshape.433
  109.2 0.7 reshape.429
  110.0 2.0 fusion.31
  112.0 0.9 copy.47
  113.5 0.9 copy.48
  114.4 0.6 convolution_convert_fusion.7
  115.0 0.9 copy.49
  115.9 1.8 fusion.91
  118.3 0.6 log_add_fusion
  118.9 0.7 fusion.33
  119.6 0.7 copy-done.7
  120.3 0.6 fusion.92
  121.3 8.3 %multiply_convert_fusion.1 = (bf16[256,3072]{1,0:T(8,128)(2,1)S(1)}, f32[256,3072]{1,0:T(8,128)S(1)}, f32[256,3072]{1,0:T(8,128)S(1)}) fusion(f32[3072]{0:T(1024)S(1)} %copy-done.31, bf16[768,3072]{1,0:T(8,128)(2,1)S(1)} %bitcast.162, f32[256,768]{1,0:T(8,128)S(1)} %get-tuple-element.78, f32[768]{0:T(1024)S(1)} %reshape.431, f32[768]{0:T(1024)S(1)} %reshape.430, ...), kind=kOutput, calls=%fused_computation.11 | convolution fusion | flops 1260847104 | bytes 13389824 | tf_op jit(solution)/shard_map/dot_general | solution.py:28
  129.6 2.7 fusion.95
  132.3 2.2 fusion.30
  134.5 3.0 %multiply_reduce_fusion.1 = (bf16[768]{0:T(1024)(128)(2,1)}, f32[256]{0:T(256)}, bf16[768]{0:T(1024)(128)(2,1)}, f32[256,768]{1,0:T(8,128)}) fusion(f32[256,768]{1,0:T(8,128)S(1)} %get-tuple-element.78, f32[256]{0:T(256)S(1)} %fusion.75, f32[256]{0:T(256)S(1)} %broadcast_multiply_fusion, f32[768]{0:T(1024)S(1)} %reshape.430, ...), kind=kOutput, calls=%fused_computation.75 | convolution fusion | flops 1209530624 | bytes 7873536 | tf_op jit(solution)/shard_map/dot_general | solution.py:38
  137.6 1.3 convert_element_type.400
  138.9 0.6 multiply_multiply_fusion.6
  139.5 1.7 fusion.89
  141.3 0.9 copy-done.3
  142.7 2.7 convolution_convert_fusion.6
  145.4 1.9 copy.51
  147.3 1.3 convert_element_type.402
  148.6 1.3 reshape.416
  149.9 1.3 copy.55
  151.2 3.0 bitcast_reduce_fusion
  154.2 1.3 stack_reshape.5
  155.5 3.2 %convolution_convert_fusion.2 = bf16[768,768]{1,0:T(8,128)(2,1)} fusion(bf16[256,768]{0,1:T(8,128)(2,1)} %bitcast.128, f32[256,768]{1,0:T(8,128)} %copy-done.3, bf16[256,768]{1,0:T(8,128)(2,1)} %param.20, f32[256]{0:T(256)} %copy-done.27, f32[256]{0:T(256)S(1)} %compare_convert_fusion), kind=kOutput, calls=%fused_computation.39 | convolution fusion | flops 303562752 | bytes 2754560 | tf_op jit(solution)/shard_map/dot_general | solution.py:32
  158.7 2.7 convolution_convert_fusion.3
  161.4 4.4 %convolution_convert_fusion.1 = bf16[768,3072]{1,0:T(8,128)(2,1)} fusion(bf16[256,3072]{1,0:T(8,128)(2,1)S(1)} %copy-done.14, f32[256,768]{1,0:T(8,128)S(1)} %copy-done.1, f32[768]{0:T(1024)S(1)} %reshape.431, f32[768]{0:T(1024)S(1)} %reshape.430, f32[256]{0:T(256)} %copy-done.30, f32[256]{0:T(256)} %copy-done.25), kind=kOutput, calls=%fused_computation.2 | convolution fusion | flops 1211301888 | bytes 7086080 | tf_op jit(solution)/shard_map/dot_general | solution.py:32
  165.8 2.3 fusion.96
  168.1 5.2 %fusion.40 = bf16[12,64,256]{2,1,0:T(8,128)(2,1)} fusion(bf16[256,12,64]{0,2,1:T(8,128)(2,1)} %bitcast.136, f32[12,256,256]{1,2,0:T(8,128)} %fusion.96, f32[12,256,256]{1,2,0:T(8,128)S(1)} %get-tuple-element.76, f32[12,256]{1,0:T(8,128)} %log_add_fusion), kind=kOutput, calls=%fused_computation.57 | convolution fusion | flops 106368256 | bytes 7090176 | tf_op jit(solution)/shard_map/hqk,qhd->khd/dot_general | solution.py:135
  173.4 5.0 %bitcast_reduce_fusion.1 = (bf16[12,64]{1,0:T(8,128)(2,1)S(1)}, bf16[12,64,256]{2,1,0:T(8,128)(2,1)}) fusion(bf16[256,12,64]{0,2,1:T(8,128)(2,1)} %bitcast.134, f32[12,256,256]{1,2,0:T(8,128)} %fusion.96, f32[12,256,256]{1,2,0:T(8,128)S(1)} %get-tuple-element.76, f32[12,256]{1,0:T(8,128)} %log_add_fusion), kind=kOutput, calls=%fused_computation.87 | convolution fusion | flops 106564096 | bytes 7091712 | tf_op jit(solution)/shard_map/hqk,khd->qhd/dot_general | solution.py:131
  178.4 2.1 fusion.97
  180.5 1.5 convolution_add_fusion.2
  182.2 0.6 fusion.88
  183.5 1.3 fusion.54
  185.2 1.7 convolution_convert_fusion.4
  186.9 1.7 convolution_convert_fusion.5
  188.6 3.7 %convolution_convert_fusion = bf16[3072,768]{1,0:T(8,128)(2,1)} fusion(bf16[256,3072]{1,0:T(8,128)(2,1)S(1)} %copy-done.9, bf16[256,768]{1,0:T(8,128)(2,1)S(1)} %copy-done.6, f32[256]{0:T(256)S(1)} %compare_convert_fusion), kind=kOutput, calls=%fused_computation.1 | convolution fusion | flops 1210908672 | bytes 6685696 | tf_op jit(solution)/shard_map/dot_general | solution.py:32
  192.3 100.6 %reduce_gradients.1 = (bf16[2,3,16,128]{3,2,1,0:T(8,128)(2,1)S(1)}, bf16[2,3,16,768]{3,2,1,0:T(8,128)(2,1)S(1)}, bf16[2,3,16,768]{3,2,1,0:T(8,128)(2,1)S(1)}, bf...) custom-call(bf16[4,2,2,3,16,128]{5,4,3,2,1,0:T(8,128)(2,1)S(1)} %bit, ...), custom_call_target="tpu_custom_call" | custom-call | tf_op jit(solution)/shard_map/reduce_gradients/pallas_call | solution.py:463
  292.9 0.6 slice_bitcast_fusion
  294.0 0.9 bitcast_convert_fusion.4
  294.9 0.9 bitcast_convert_fusion.2
  295.7 1.2 bitcast_convert_fusion.1
  296.9 1.1 bitcast_convert_fusion
  (129 shorter events, 3.9 us)
Async XLA Ops:
  8.5 104.5 %copy-start.2 = (bf16[256,768]{1,0:T(8,128)(2,1)S(1)}, bf16[256,768]{1,0:T(8,128)(2,1)}, u32[]{:S(2)}) copy-start(bf16[256,768]{1,0:T(8,128)(2,1)} %param.18) | copy-start | bytes 1179652
  8.5 105.9 %copy-start.23 = (f32[256]{0:T(256)}, f32[256]{0:T(256)S(1)}, u32[]{:S(2)}) copy-start(f32[256]{0:T(256)S(1)} %broadcast_multiply_fusion.1) | copy-start | bytes 3076
  9.8 95.7 %copy-start.34 = (f32[256]{0:T(256)}, f32[256]{0:T(256)S(1)}, u32[]{:S(2)}) copy-start(f32[256]{0:T(256)S(1)} %fusion.52) | copy-start | bytes 3076
  9.8 104.6 %copy-start.32 = (f32[256]{0:T(256)}, f32[256]{0:T(256)S(1)}, u32[]{:S(2)}) copy-start(f32[256]{0:T(256)S(1)} %fusion.74) | copy-start | bytes 3076
  105.4 7.5 %copy-start.20 = (bf16[4,2,2,3,16,768]{5,4,3,2,1,0:T(8,128)(2,1)S(1)}, bf16[4,2,2,3,16,768]{5,4,3,2,1,0:T(8,128)(2,1)}, u32[]{:S(2)}) copy-start(bf16[4,2,2,3,16,768]{5,4,3,2,1,0:T(8,128)(2,1)} %get-tuple-element.33) | copy-start | bytes 3538948
  109.0 5.4 %copy-start.40 = (f32[768]{0:T(1024)}, f32[768]{0:T(1024)S(1)}, u32[]{:S(2)}) copy-start(f32[768]{0:T(1024)S(1)} %reshape.426) | copy-start | bytes 9220
  110.0 4.5 %copy-start.18 = (bf16[4,2,2,3,16,768]{5,4,3,2,1,0:T(8,128)(2,1)S(1)}, bf16[4,2,2,3,16,768]{5,4,3,2,1,0:T(8,128)(2,1)}, u32[]{:S(2)}) copy-start(bf16[4,2,2,3,16,768]{5,4,3,2,1,0:T(8,128)(2,1)} %get-tuple-element.34) | copy-start | bytes 3538948
  115.9 2.9 copy-start.15
  117.8 3.4 %slice-start = ((s8[4718592]{0:T(1024)(128)(4,1)}), s8[4194304]{0:T(1024)(128)(4,1)S(1)}, s32[]{:S(2)}) async-start(s8[4718592]{0:T(1024)(128)(4,1)} %bitcast.160), calls=%async_computation | async-start | bytes 8388608
  118.9 1.5 copy-start.7
  118.9 1.5 copy-start.29
  118.9 2.3 slice-start.1
  119.6 1.6 copy-start.11
  119.6 1.7 copy-start.31
  120.3 9.2 %slice-start.2 = ((s8[4718592]{0:T(1024)(128)(4,1)}), s8[4194304]{0:T(1024)(128)(4,1)S(1)}, s32[]{:S(2)}) async-start(s8[4718592]{0:T(1024)(128)(4,1)} %bitcast.164), calls=%async_computation.2 | async-start | bytes 8388608
  120.9 13.6 %copy-start = (f32[256,768]{1,0:T(8,128)}, f32[256,768]{1,0:T(8,128)S(1)}, u32[]{:S(2)}) copy-start(f32[256,768]{1,0:T(8,128)S(1)} %get-tuple-element.78) | copy-start | bytes 2359300
  121.0 13.5 %copy-start.25 = (f32[256]{0:T(256)}, f32[256]{0:T(256)S(1)}, u32[]{:S(2)}) copy-start(f32[256]{0:T(256)S(1)} %broadcast_multiply_fusion) | copy-start | bytes 3076
  121.2 8.4 %copy-start.36 = (f32[256]{0:T(256)}, f32[256]{0:T(256)S(1)}, u32[]{:S(2)}) copy-start(f32[256]{0:T(256)S(1)} %multiply_reduce_fusion.3) | copy-start | bytes 3076
  121.3 13.2 %copy-start.30 = (f32[256]{0:T(256)}, f32[256]{0:T(256)S(1)}, u32[]{:S(2)}) copy-start(f32[256]{0:T(256)S(1)} %fusion.75) | copy-start | bytes 3076
  121.3 8.3 %copy-start.5 = (bf16[256,768]{1,0:T(8,128)(2,1)S(1)}, bf16[256,768]{1,0:T(8,128)(2,1)}, u32[]{:S(2)}) copy-start(bf16[256,768]{1,0:T(8,128)(2,1)} %param.20) | copy-start | bytes 1179652
  121.3 8.3 %slice-start.3 = ((s8[4718592]{0:T(1024)(128)(4,1)}), s8[524288]{0:T(1024)(128)(4,1)S(1)}, s32[]{:S(2)}) async-start(s8[4718592]{0:T(1024)(128)(4,1)} %bitcast.164), calls=%async_computation.3 | async-start | bytes 1048576
  129.6 2.8 copy-start.8
  129.6 2.7 copy-start.42
  132.3 2.2 copy-start.13
  141.2 0.9 copy-start.3
  142.1 0.5 copy-start.27
  155.5 5.9 %copy-start.1 = (f32[256,768]{1,0:T(8,128)S(1)}, f32[256,768]{1,0:T(8,128)}, u32[]{:S(2)}) copy-start(f32[256,768]{1,0:T(8,128)} %copy-done) | copy-start | bytes 2359300
  155.5 5.9 %copy-start.14 = (bf16[256,3072]{1,0:T(8,128)(2,1)S(1)}, bf16[256,3072]{1,0:T(8,128)(2,1)}, u32[]{:S(2)}) copy-start(bf16[256,3072]{1,0:T(8,128)(2,1)} %copy-done.13) | copy-start | bytes 4718596
  161.4 4.5 %copy-start.10 = (bf16[256,768]{0,1:T(8,128)(2,1)S(1)}, bf16[256,768]{0,1:T(8,128)(2,1)}, u32[]{:S(2)}) copy-start(bf16[256,768]{0,1:T(8,128)(2,1)} %copy.51) | copy-start | bytes 1179652
  161.4 4.5 %copy-start.16 = (bf16[256,768]{0,1:T(8,128)(2,1)S(1)}, bf16[256,768]{0,1:T(8,128)(2,1)}, u32[]{:S(2)}) copy-start(bf16[256,768]{0,1:T(8,128)(2,1)} %copy.47) | copy-start | bytes 1179652
  178.3 2.2 copy-start.19
  178.4 3.7 %copy-start.12 = (bf16[12,64,256]{2,1,0:T(8,128)(2,1)S(1)}, bf16[12,64,256]{2,1,0:T(8,128)(2,1)}, u32[]{:S(2)}) copy-start(bf16[12,64,256]{2,1,0:T(8,128)(2,1)} %get-tuple-element.85) | copy-start | bytes 1179652
  178.4 3.7 %copy-start.24 = (f32[256]{0:T(256)S(1)}, f32[256]{0:T(256)}, u32[]{:S(2)}) copy-start(f32[256]{0:T(256)} %copy-done.23) | copy-start | bytes 3076
  178.4 3.6 %copy-start.17 = (bf16[4,2,2,3,16,768]{5,4,3,2,1,0:T(8,128)(2,1)S(1)}, bf16[4,2,2,3,16,768]{5,4,3,2,1,0:T(8,128)(2,1)}, u32[]{:S(2)}) copy-start(bf16[4,2,2,3,16,768]{5,4,3,2,1,0:T(8,128)(2,1)} %get-tuple-element.32) | copy-start | bytes 3538948
  180.5 2.3 copy-start.35
  180.5 2.4 copy-start.33
  182.1 1.4 copy-start.4
  182.1 1.4 copy-start.6
  182.1 1.4 copy-start.28
  182.1 2.9 copy-start.37
  182.1 2.9 copy-start.38
  182.1 2.9 copy-start.39
  182.2 3.0 copy-start.26
  182.8 2.4 copy-start.22
  182.8 2.4 copy-start.41
  182.9 4.0 %copy-start.21 = (bf16[12,64,256]{2,1,0:T(8,128)(2,1)S(1)}, bf16[12,64,256]{2,1,0:T(8,128)(2,1)}, u32[]{:S(2)}) copy-start(bf16[12,64,256]{2,1,0:T(8,128)(2,1)} %get-tuple-element.83) | copy-start | bytes 1179652
  184.8 3.7 %copy-start.9 = (bf16[256,3072]{1,0:T(8,128)(2,1)S(1)}, bf16[256,3072]{1,0:T(8,128)(2,1)}, u32[]{:S(2)}) copy-start(bf16[256,3072]{1,0:T(8,128)(2,1)} %copy-done.8) | copy-start | bytes 4718596

commit v2 on v1

--- a/solution.py
+++ b/solution.py
@@ -44,11 +44,68 @@
     return jnp.sum(values.astype(jnp.float32), axis=0)
 
 
-def masked_scores(heads_q, heads_k, allowed):
-    scores = jnp.einsum(
-        "qhd,khd->hqk", heads_q, heads_k, preferred_element_type=jnp.float32
-    ) * HEAD_DIM ** (-0.5)
-    return jnp.where(allowed[None], scores, -1e30)
+def head_probs(query, keys, allowed):
+    scores = against(query, keys) * HEAD_DIM ** (-0.5)
+    scores = jnp.where(allowed, scores, -1e30)
+    expo = jnp.exp(scores - jnp.max(scores, axis=-1, keepdims=True))
+    return expo / jnp.sum(expo, axis=-1, keepdims=True)
+
+
+def allowed_pairs(seg_col, seg_row):
+    count = seg_col.shape[0]
+    row = lax.broadcasted_iota(jnp.int32, (count, count), 0)
+    col = lax.broadcasted_iota(jnp.int32, (count, count), 1)
+    return (seg_col[...] == seg_row[...]) & (row >= col)
+
+
+def attend_kernel(seg_col, seg_row, query, keys, values, mixed):
+    allowed = allowed_pairs(seg_col, seg_row)
+    for first in range(0, HEADS, 2):
+        parts = []
+        for head in (first, first + 1):
+            at = slice(head * HEAD_DIM, (head + 1) * HEAD_DIM)
+            probs = head_probs(query[:, at], keys[:, at], allowed)
+            parts.append(product(probs.astype(jnp.bfloat16), values[:, at]))
+        at = slice(first * HEAD_DIM, (first + 2) * HEAD_DIM)
+        mixed[:, at] = jnp.concatenate(parts, axis=1).astype(jnp.bfloat16)
+
+
+def attend_back_kernel(
+    seg_col, seg_row, query, keys, values, grad_mixed, grad_query, grad_keys, grad_values
+):
+    allowed = allowed_pairs(seg_col, seg_row)
+    for first in range(0, HEADS, 2):
+        parts = []
+        for head in (first, first + 1):
+            at = slice(head * HEAD_DIM, (head + 1) * HEAD_DIM)
+            q, k, v, g = query[:, at], keys[:, at], values[:, at], grad_mixed[:, at]
+            probs = head_probs(q, k, allowed)
+            grad_probs = against(g, v)
+            inner_sum = jnp.sum(grad_probs * probs, axis=-1, keepdims=True)
+            grad_scores = (probs * (grad_probs - inner_sum) * HEAD_DIM ** (-0.5)).astype(
+                jnp.bfloat16
+            )
+            parts.append(
+                (
+                    product(grad_scores, k),
+                    inner(grad_scores, q),
+                    inner(probs.astype(jnp.bfloat16), g),
+                )
+            )
+        at = slice(first * HEAD_DIM, (first + 2) * HEAD_DIM)
+        for ref, left, right in zip((grad_query, grad_keys, grad_values), *parts):
+            ref[:, at] = jnp.concatenate([left, right], axis=1).astype(jnp.bfloat16)
+
+
+def local_call(kernel, outputs, seg_ids, *arrays):
+    vmem = pl.BlockSpec(memory_space=pltpu.VMEM)
+    return pl.pallas_call(
+        kernel,
+        out_shape=[jax.ShapeDtypeStruct(arrays[0].shape, jnp.bfloat16)] * outputs,
+        in_specs=[vmem] * (2 + len(arrays)),
+        out_specs=[vmem] * outputs,
+        compiler_params=pltpu.CompilerParams(vmem_limit_bytes=32 * 1024 * 1024),
+    )(seg_ids[:, None], seg_ids[None, :], *arrays)
 
 
 def layer(tokens, seg_ids, grad_out, gathered):
@@ -70,27 +127,13 @@
         b_two,
     ) = gathered
     rows = tokens.astype(jnp.float32)
-    count = rows.shape[0]
-    width = rows.shape[1]
-    order = jnp.arange(count)
-    allowed = (seg_ids[:, None] == seg_ids[None, :]) & (order[:, None] >= order[None, :])
     gain_first = gain_one.astype(jnp.float32)
     shift_first = shift_one.astype(jnp.float32)
     normed = layer_norm(rows, gain_first, shift_first).astype(jnp.bfloat16)
     query = (product(normed, wq) + bq.astype(jnp.float32)).astype(jnp.bfloat16)
     keys = product(normed, wk).astype(jnp.bfloat16)
     values = (product(normed, wv) + bv.astype(jnp.float32)).astype(jnp.bfloat16)
-    heads_q = query.reshape(count, HEADS, HEAD_DIM)
-    heads_k = keys.reshape(count, HEADS, HEAD_DIM)
-    heads_v = values.reshape(count, HEADS, HEAD_DIM)
-    scores = masked_scores(heads_q, heads_k, allowed)
-    peak = jnp.max(scores, axis=-1, keepdims=True)
-    expo = jnp.exp(scores - peak)
-    total = jnp.sum(expo, axis=-1, keepdims=True)
-    logsum = peak + jnp.log(total)
-    probs_low = (expo / total).astype(jnp.bfloat16)
-    mixed = jnp.einsum("hqk,khd->qhd", probs_low, heads_v, preferred_element_type=jnp.float32)
-    mixed = mixed.reshape(count, width).astype(jnp.bfloat16)
+    (mixed,) = local_call(attend_kernel, 1, seg_ids, query, keys, values)
     middle = rows + product(mixed, wo) + bo.astype(jnp.float32)
     gain_second = gain_two.astype(jnp.float32)
     shift_second = shift_two.astype(jnp.float32)
@@ -104,41 +147,28 @@
     upstream = grad_out.astype(jnp.float32) * live
     grad_b_two = jnp.sum(upstream, axis=0)
     up_low = upstream.astype(jnp.bfloat16)
-    grad_w_two = inner(active, up_low)
+    grad_w_two = (active, up_low)
     grad_active = against(up_low, back_w_two)
     gelu_out, gelu_pull = jax.vjp(gelu_exact, hidden)
     grad_hidden = gelu_pull(grad_active)[0].astype(jnp.bfloat16)
     grad_b_one = column_sum(grad_hidden)
-    grad_w_one = inner(normed_two, grad_hidden)
+    grad_w_one = (normed_two, grad_hidden)
     grad_normed_two = against(grad_hidden, back_w_one)
     norm_out, norm_pull = jax.vjp(layer_norm, middle, gain_second, shift_second)
     grad_mid_norm, grad_gain_two, grad_shift_two = norm_pull(grad_normed_two)
     grad_middle = upstream + grad_mid_norm
     grad_bo = jnp.sum(grad_middle, axis=0)
     mid_low = grad_middle.astype(jnp.bfloat16)
-    grad_wo = inner(mixed, mid_low)
-    grad_mixed = against(mid_low, back_wo).astype(jnp.bfloat16).reshape(count, HEADS, HEAD_DIM)
-    scores_again = masked_scores(heads_q, heads_k, allowed)
-    probs = jnp.exp(scores_again - logsum)
-    probs_again = probs.astype(jnp.bfloat16)
-    grad_probs = jnp.einsum("qhd,khd->hqk", grad_mixed, heads_v, preferred_element_type=jnp.float32)
-    grad_values = jnp.einsum(
-        "hqk,qhd->khd", probs_again, grad_mixed, preferred_element_type=jnp.float32
-    )
-    grad_values = grad_values.reshape(count, width).astype(jnp.bfloat16)
-    inner_sum = jnp.sum(grad_probs * probs, axis=-1, keepdims=True)
-    grad_scores = (probs * (grad_probs - inner_sum) * HEAD_DIM ** (-0.5)).astype(jnp.bfloat16)
-    grad_query = jnp.einsum(
-        "hqk,khd->qhd", grad_scores, heads_k, preferred_element_type=jnp.float32
-    )
-    grad_query = grad_query.reshape(count, width).astype(jnp.bfloat16)
-    grad_keys = jnp.einsum("hqk,qhd->khd", grad_scores, heads_q, preferred_element_type=jnp.float32)
-    grad_keys = grad_keys.reshape(count, width).astype(jnp.bfloat16)
+    grad_wo = (mixed, mid_low)
+    grad_mixed = against(mid_low, back_wo).astype(jnp.bfloat16)
+    grad_query, grad_keys, grad_values = local_call(
+        attend_back_kernel, 3, seg_ids, query, keys, values, grad_mixed
+    )
     grad_bq = column_sum(grad_query)
     grad_bv = column_sum(grad_values)
-    grad_wq = inner(normed, grad_query)
-    grad_wk = inner(normed, grad_keys)
-    grad_wv = inner(normed, grad_values)
+    grad_wq = (normed, grad_query)
+    grad_wk = (normed, grad_keys)
+    grad_wv = (normed, grad_values)
     grad_normed = (
         against(grad_query, back_wq) + against(grad_keys, back_wk) + against(grad_values, back_wv)
     )
@@ -167,6 +197,7 @@
 def on_device_plain(tokens, seg_ids, grad_out, *params):
     gathered = tuple(lax.all_gather(p, "shard", axis=0, tiled=True) for p in params)
     result, grad_input, grads = layer(tokens, seg_ids, grad_out, gathered)
+    grads = tuple(inner(*g) if isinstance(g, tuple) else g for g in grads)
     owned = tuple(
         lax.psum_scatter(g, "shard", scatter_dimension=0, tiled=True) for g in grads
     )
@@ -177,6 +208,8 @@
 HALVES = 2
 THIRDS = 3
 MESH = pl.DeviceIdType.MESH
+GATHER_PIECE, GATHER_AHEAD, GATHER_LAGS = 16 * 768, 4, (2, 4)
+REDUCE_LAGS = (0, 2, 4, 6, 8, 10)
 
 
 def place():
@@ -267,21 +300,25 @@
         by_y.append(remote(ref, ref, ys.at[a], yr.at[a], device(1 - y, core, z, x)))
         ref = part(out, piece, slice(None), slice(None), core, slice(None))
         by_core.append(remote(ref, ref, cs.at[a], cr.at[a], device(y, 1 - core, z, x)))
-    for copies in by_z:
+    for copies in by_z[:GATHER_AHEAD]:
         for copy in copies:
             copy.start()
-    for step in range(total + 2):
-        if 0 <= step - 2 < total:
-            by_y[step - 2].wait_recv()
-            by_core[step - 2].start()
-        if 0 <= step - 1 < total:
-            by_x[step - 1].wait_recv()
-            by_y[step - 1].start()
+    x_lag, y_lag = GATHER_LAGS
+    for step in range(total + y_lag):
+        if 0 <= step - y_lag < total:
+            by_y[step - y_lag].wait_recv()
+            by_core[step - y_lag].start()
+        if 0 <= step - x_lag < total:
+            by_x[step - x_lag].wait_recv()
+            by_y[step - x_lag].start()
         if step < total:
             own[step].wait()
             for copy in by_z[step]:
                 copy.wait_recv()
             by_x[step].start()
+            if step + GATHER_AHEAD < total:
+                for copy in by_z[step + GATHER_AHEAD]:
+                    copy.start()
     for a in range(total):
         by_core[a].wait_recv()
     for a in range(total):
@@ -294,7 +331,7 @@
 
 def gather_all(shards):
     shapes = [s.shape[2:] for s in shards]
-    pieces = cut(shapes, 16 * 1536)
+    pieces = cut(shapes, GATHER_PIECE)
     total, count = len(pieces), len(shards)
     dma = pltpu.SemaphoreType.DMA
     return pl.pallas_call(
@@ -313,13 +350,14 @@
     )(*shards)
 
 
-def reduce_kernel(pieces, count, *refs):
-    ins, outs = refs[:count], refs[count : 2 * count]
+def reduce_kernel(pieces, factors, operands, small, *refs):
+    ins, outs = refs[:operands], refs[operands : operands + len(factors) + 1]
     total = len(pieces)
-    bufs = refs[2 * count : 2 * count + 5 * total]
-    one, two, three, four, five = [bufs[i * total : (i + 1) * total] for i in range(5)]
-    done = refs[2 * count + 5 * total : 2 * count + 6 * total]
-    sems = refs[2 * count + 6 * total :]
+    bufs = refs[operands + len(factors) + 1 :]
+    sems = bufs[7 * total :]
+    terms, one, two, three, four, five, done = [
+        bufs[i * total : (i + 1) * total] for i in range(7)
+    ]
     cs, cr, ys, yr, xs, xr, zs, zr, us, ur, fs, fr = sems
     y, core, z, x = place()
     f32, b16 = jnp.float32, jnp.bfloat16
@@ -333,7 +371,7 @@
     for a, piece in enumerate(pieces):
         by_core.append(
             remote(
-                part(ins[piece[0]], piece, every, every, 1 - core, every),
+                terms[a].at[:, :, 1 - core],
                 one[a],
                 cs.at[a],
                 cr.at[a],
@@ -378,9 +416,24 @@
             remote(final, final, fs.at[a], fr.at[a], device(y, 1 - core, z, x))
         )
 
+    def make(a):
+        at, _, _, c, cols = pieces[a]
+        if at == 0:
+            terms[a][...] = small[...]
+        else:
+            left, right = factors[at - 1]
+            term = lax.dot_general(
+                ins[left][...],
+                ins[right][:, c : c + cols],
+                (((0,), (0,)), ((), ())),
+                preferred_element_type=f32,
+            )
+            terms[a][...] = term.reshape(terms[a].shape).astype(b16)
+        by_core[a].start()
+
     def add_core(a):
         by_core[a].wait_recv()
-        mine = part(ins[pieces[a][0]], pieces[a], every, every, core, every)
+        mine = terms[a].at[:, :, core]
 
         @pl.loop(0, 8)
         def _(s):
@@ -431,13 +484,11 @@
         back_core[a].start()
 
     greet(y, core, z, x)
-    for a in range(total):
-        by_core[a].start()
-    stages = (add_core, add_y, add_x, add_z, add_planes)
-    for step in range(total + len(stages) - 1):
-        for late in reversed(range(len(stages))):
-            if 0 <= step - late < total:
-                stages[late](step - late)
+    stages = (make, add_core, add_y, add_x, add_z, add_planes)
+    for step in range(total + REDUCE_LAGS[-1]):
+        for stage, lag in zip(reversed(stages), reversed(REDUCE_LAGS)):
+            if 0 <= step - lag < total:
+                stage(step - lag)
     for a in range(total):
         back_core[a].wait_recv()
     for a in range(total):
@@ -450,27 +501,46 @@
         back_core[a].wait_send()
 
 
-def reduce_all(grads):
-    shapes = [g.shape[4:] for g in grads]
-    pieces = cut(shapes, 16 * 1536)
-    total, count = len(pieces), len(grads)
+def reduce_all(small, pairs):
+    operands, factors = [], []
+    for pair in pairs:
+        for value in pair:
+            if not any(value is other for other in operands):
+                operands.append(value)
+        factors.append(
+            tuple([value is other for other in operands].index(True) for value in pair)
+        )
+    shards = 8 * HALVES * THIRDS
+    shapes = [small.shape[4:]] + [(l.shape[1] // shards, r.shape[1]) for l, r in pairs]
+    pieces = []
+    for at, (rows, cols) in enumerate(shapes):
+        step = min(cols, 768 if rows == 16 else 256)
+        pieces += [(at, 0, rows, c, step) for c in range(0, cols, step)]
+    total = len(pieces)
     dma = pltpu.SemaphoreType.DMA
-    leads = ((4, 2, 3), (4, 2), (4, 2), (3, 2), (2,), (2,))
+    leads = ((4, 2, HALVES, 3), (4, 2, 3), (4, 2), (4, 2), (3, 2), (2,), (2,))
     buffers = [
         pltpu.VMEM(lead + (p[2], p[4]), jnp.bfloat16) for lead in leads for p in pieces
     ]
     single, triple = dma((total,)), dma((total, 3))
+    vmem = pl.BlockSpec(memory_space=pltpu.VMEM)
+
+    def kernel(small_ref, *refs):
+        reduce_kernel(pieces, factors, len(operands), small_ref, *refs)
+
     return pl.pallas_call(
-        functools.partial(reduce_kernel, pieces, count),
-        out_shape=[jax.ShapeDtypeStruct(g.shape[2:], g.dtype) for g in grads],
-        in_specs=[pl.BlockSpec(memory_space=pltpu.VMEM)] * count,
-        out_specs=[pl.BlockSpec(memory_space=pltpu.VMEM)] * count,
+        kernel,
+        out_shape=[
+            jax.ShapeDtypeStruct((HALVES, THIRDS) + shape, jnp.bfloat16) for shape in shapes
+        ],
+        in_specs=[vmem] * (1 + len(operands)),
+        out_specs=[vmem] * len(shapes),
         scratch_shapes=buffers + [single] * 6 + [triple] * 2 + [single] * 4,
         compiler_params=pltpu.CompilerParams(
-            collective_id=1, has_side_effects=True, vmem_limit_bytes=52 * 1024 * 1024
+            collective_id=1, has_side_effects=True, vmem_limit_bytes=56 * 1024 * 1024
         ),
         name="reduce_gradients",
-    )(*grads)
+    )(small, *operands)
 
 
 VECTORS = (0, 1, 5, 6, 8, 9, 10, 14)
@@ -503,19 +573,14 @@
 
     result, grad_input, grads = layer(tokens, seg_ids, grad_out, gathered)
 
-    low = [g.astype(jnp.bfloat16) for g in grads]
+    low = {i: grads[i].astype(jnp.bfloat16) for i in VECTORS + (B_ONE,)}
     vectors = jnp.stack([low[i].reshape(8, width) for i in VECTORS], axis=1)
     vectors = jnp.pad(vectors, ((0, 0), (0, 0), (0, lanes - width)))
     vectors = jnp.concatenate([vectors, low[B_ONE].reshape(8, many, lanes)], axis=1)
     vectors = jnp.pad(vectors, ((0, 0), (0, rows - vectors.shape[1]), (0, 0)))
     shapes = [(rows, lanes)] + [params[i].shape for i in MATRICES]
-    arrays = [vectors] + [low[i] for i in MATRICES]
-    sums = reduce_all(
-        [
-            g.reshape(4, 2, HALVES, THIRDS, shape[0] // 6, shape[1])
-            for g, shape in zip(arrays, shapes)
-        ]
-    )
+    vectors = vectors.reshape(4, 2, HALVES, THIRDS, rows // 6, lanes)
+    sums = reduce_all(vectors, [grads[i] for i in MATRICES])
     sums = [s.reshape(shape).astype(jnp.float32) for s, shape in zip(sums, shapes)]
     owned = [None] * len(params)
     for at, i in enumerate(VECTORS):

time: 299 us -> 242 us (0.81)
  matrix products: 62.1 us -> 24.1 us
  Pallas kernels: 194 us -> 180 us
  local copies, waits for them, and re-layouts: 24.3 us -> 12.9 us
  other arithmetic: 16.2 us -> 23.1 us
    dot_general x12 -> x0, matrix products: 35.3 us -> none  [the longest x6 17.3 us: inner(): lax.dot_general(left, right, (((0,), (0,)), ((), ())), preferred_element_...]
    pallas_call x1, Pallas kernels: 93.5 us -> 79 us  [gather_all(): pl.pallas_call(functools.partial(gather_kernel, pieces, count), out_shape...]
    convert_element_type x0 -> x5, other arithmetic: none -> 6.29 us  [the longest x1 3.43 us: layer(): active = gelu_exact(hidden).astype(jnp.bfloat16)]
    dot_general x6, matrix products: 14.2 us -> 8.35 us  [product(): return jnp.dot(left, right, preferred_element_type=jnp.float32)]
    convert_element_type x8 -> x6, local copies, waits for them, and re-layouts: 5.85 us -> 0.51 us  [on_device(): low = {i: grads[i].astype(jnp.bfloat16) for i in VECTORS + (B_ONE,)}]
    convert_element_type x5, other arithmetic: 4.03 us -> 7.77 us  [on_device(): s.reshape(shape).astype(jnp.float32)]
    dot_general x6, matrix products: 12.6 us -> 15.7 us  [against(): lax.dot_general(left, right, (((1,), (1,)), ((), ())), preferred_element_...]
    pallas_call x1 -> x3, Pallas kernels: 101 us -> 101 us  [the longest x1 89.8 us: reduce_all(): pl.pallas_call(kernel, out_shape=[jax.ShapeDtypeStruct((HALVES, THIRDS) +...]
where the time goes in v2:
time: 242 us; the launch traced here: 241 us
  Pallas kernels  180 us (74%)
  matrix products  24.1 us (10%)
  other arithmetic  23.1 us (10%)
  local copies, waits for them, and re-layouts  12.9 us (5%)
    pallas_call x1, Pallas kernels, reduce_all(): pl.pallas_call(kernel, out_shape=[jax.ShapeDtypeStruct((HALVES, THIRDS) +...  89.8 us
    pallas_call x1, Pallas kernels, gather_all(): pl.pallas_call(functools.partial(gather_kernel, pieces, count), out_shape...  79 us
    dot_general x6, matrix products, against(): lax.dot_general(left, right, (((1,), (1,)), ((), ())), preferred_element_...  15.7 us
    pallas_call x2, Pallas kernels, local_call(): pl.pallas_call(kernel, out_shape=[jax.ShapeDtypeStruct(arrays[0].shape, j...  10.8 us
    dot_general x6, matrix products, product(): return jnp.dot(left, right, preferred_element_type=jnp.float32)  8.35 us
    convert_element_type x5, other arithmetic, on_device(): s.reshape(shape).astype(jnp.float32)  7.77 us
    pad x8, local copies, waits for them, and re-layouts, on_device(): jnp.pad(params[i][None], ((0, 0), (0, lanes - width)))  5.34 us

profile of v2, /device:TPU:1, one launch (start us, length us, event | category | flops | bytes accessed | tf_op | source)
XLA Modules:
  0.0 241.0 jit_solution(11787341084580489797)
XLA Ops:
  0.7 0.7 pad.37
  1.4 0.7 pad.38
  2.0 0.7 pad.39
  2.7 0.7 pad.40
  3.4 0.7 pad.41
  4.0 0.7 pad.42
  4.7 0.7 pad.43
  5.3 0.7 pad.44
  6.0 0.7 concatenate.6
  6.7 0.7 compare_convert_fusion
  7.4 1.1 convert_reduce_fusion
  8.6 1.2 fusion.20
  9.8 0.6 pad.45
  10.4 0.8 copy.35.seg_col
  11.2 1.1 fusion.23.refs_9_
  12.4 79.0 %gather_parameters.1 = (bf16[4,2,2,3,16,128]{5,4,3,2,1,0:T(8,128)(2,1)}, bf16[4,2,2,3,16,768]{5,4,3,2,1,0:T(8,128)(2,1)}, bf16[4,2,2,3,16,768]{5,4,3,2,1,0:T(8,1...) custom-call(bf16[2,3,16,128]{3,2,1,0:T(8,128)(2,1)} %bitcast.107, ...), custom_call_target="tpu_custom_call" | custom-call | tf_op jit(solution)/shard_map/gather_parameters/pallas_call | solution.py:337
  91.4 0.8 slice_convert_fusion
  92.3 1.1 fusion.26
  93.4 0.1 reshape.326
  94.0 0.3 fusion.18.refs_0_
  94.3 1.9 fusion.10.values
  96.2 1.8 fusion.9.query
  98.0 0.5 convolution_convert_fusion.1.keys
  98.6 3.8 %shard_map.305.refs_4_ = bf16[256,768]{1,0:T(8,128)(2,1)S(1)} custom-call(s32[256,1]{1,0:T(8,128)S(1)} %copy.35.seg_col, s32[1,256]{1,0:T(1,128)S(1)} %bitcast.90, bf16[256,768]{1,0:T(8,128)(2,1)S(1)} %fusion.9.query, bf16[256,768]{1,0:T(8,128)(2,1)S(1)} %convolution_convert_fusion.1.keys, bf16[256,768]{1,0:T(8,128)(2,1)S(1)} %fusion.10.values), custom_call_target="tpu_custom_call" | custom-call | tf_op jit(solution)/shard_map/pallas_call | solution.py:102
  102.3 0.6 fusion.43
  102.9 0.2 multiply_reduce_fusion.2
  103.2 0.2 add_convert_fusion.1.refs_6_
  103.4 1.4 convolution_add_fusion
  104.9 0.6 slice-done
  105.5 0.1 slice-done.1
  105.6 9.8 %fusion.40 = (bf16[3072]{0:T(1024)(128)(2,1)S(1)}, bf16[256,3072]{1,0:T(8,128)(2,1)S(1)}, f32[256,3072]{1,0:T(8,128)}) fusion(f32[256,3072]{1,0:T(8,128)S(1)} %convolution_add_fusion, bf16[256,768]{1,0:T(8,128)(2,1)S(1)} %fusion.23.refs_9_, bf16[3072,768]{1,0:T(8,128)(2,1)S(1)} %bitcast.113), kind=kOutput, calls=%fused_computation.114 | convolution fusion | flops 1265366016 | bytes 12982272 | tf_op jit(solution)/shard_map/dot_general | solution.py:38
  115.5 2.4 multiply_reduce_fusion
  117.9 0.1 convert_element_type.312
  118.0 1.6 fusion.42
  119.6 3.4 %multiply_convert_fusion.refs_8_ = bf16[256,3072]{1,0:T(8,128)(2,1)S(1)} fusion(f32[256,3072]{1,0:T(8,128)} %get-tuple-element.70, f32[256,3072]{1,0:T(8,128)} %copy-done.13), kind=kLoop, calls=%fused_computation.4 | loop fusion | flops 2359296 | bytes 7864320 | tf_op jit(solution)/shard_map/convert_element_type | solution.py:142
  123.1 2.1 fusion.8
  125.3 0.1 convert_element_type.314
  125.3 1.3 fusion.38.refs_5_
  126.6 0.7 copy-done.11
  127.4 1.9 convolution_convert_fusion.grad_mixed
  129.3 7.1 %shard_map.306 = (bf16[256,768]{1,0:T(8,128)(2,1)S(1)}, bf16[256,768]{1,0:T(8,128)(2,1)S(1)}, bf16[256,768]{1,0:T(8,128)(2,1)S(1)}) custom-call(s32[256,1]{1,0:T(8,128)S(1)} %copy.35.seg_col, s32[1,256]{1,0:T(1,128)S(1)} %bitcast.91, bf16[256,768]{1,0:T(8,128)(2,1)S(1)} %fusion.9.query, bf16[256,768]{1,0:T(8,128)(2,1)S(1)} %convolution_convert_fusion.1.keys, ...), custom_call_target="tpu_custom_call" | custom-call | tf_op jit(solution)/shard_map/pallas_call | solution.py:102
  136.4 0.5 fusion.44
  136.9 0.5 convolution_add_fusion.2
  137.4 0.6 copy-done.17
  138.0 0.6 fusion.39
  138.7 0.1 convert_element_type.308
  138.8 0.1 reduce_sum.182
  138.9 0.1 stack_reshape.4
  139.0 0.1 reduce_sum.183
  139.1 0.1 stack_reshape.5
  139.1 0.7 fusion.19
  139.8 0.1 convert_element_type.306
  139.9 1.4 fusion.22
  141.2 0.1 convert_element_type.316
  141.3 0.1 convert_element_type.310
  141.5 0.7 pad.47.clone
  142.2 89.8 %reduce_gradients.1 = (bf16[2,3,16,128]{3,2,1,0:T(8,128)(2,1)}, bf16[2,3,16,768]{3,2,1,0:T(8,128)(2,1)}, bf16[2,3,16,768]{3,2,1,0:T(8,128)(2,1)}, bf16[2,3,16,76...) custom-call(bf16[4,2,2,3,16,128]{5,4,3,2,1,0:T(8,128)(2,1)} %bitcast, ...), custom_call_target="tpu_custom_call" | custom-call | tf_op jit(solution)/shard_map/reduce_gradients/pallas_call | solution.py:531
  232.1 0.8 bitcast_convert_fusion.6
  232.9 0.6 slice_bitcast_fusion
  233.5 0.5 slice_bitcast_fusion.1
  234.0 1.8 bitcast_convert_fusion.4
  235.8 1.8 bitcast_convert_fusion.2
  237.7 2.2 bitcast_convert_fusion.1
  239.9 1.1 bitcast_convert_fusion
  (76 shorter events, 0.8 us)
Async XLA Ops:
  0.7 93.3 %copy-start.5 = (bf16[256,768]{1,0:T(8,128)(2,1)S(1)}, bf16[256,768]{1,0:T(8,128)(2,1)}, u32[]{:S(2)}) copy-start(bf16[256,768]{1,0:T(8,128)(2,1)} %param.18) | copy-start | bytes 1179652
  12.4 92.5 %copy-start.14 = (bf16[256,768]{1,0:T(8,128)(2,1)}, bf16[256,768]{1,0:T(8,128)(2,1)S(1)}, u32[]{:S(2)}) copy-start(bf16[256,768]{1,0:T(8,128)(2,1)S(1)} %fusion.23.refs_9_) | copy-start | bytes 1179652
  91.4 6.6 %copy-start.7 = (bf16[4,2,2,3,16,768]{5,4,3,2,1,0:T(8,128)(2,1)S(1)}, bf16[4,2,2,3,16,768]{5,4,3,2,1,0:T(8,128)(2,1)}, u32[]{:S(2)}) copy-start(bf16[4,2,2,3,16,768]{5,4,3,2,1,0:T(8,128)(2,1)} %get-tuple-element.36) | copy-start | bytes 3538948
  94.2 3.8 %copy-start.10 = (bf16[256,768]{1,0:T(8,128)(2,1)}, bf16[256,768]{1,0:T(8,128)(2,1)S(1)}, u32[]{:S(2)}) copy-start(bf16[256,768]{1,0:T(8,128)(2,1)S(1)} %fusion.18.refs_0_) | copy-start | bytes 1179652
  94.2 4.3 %copy-start.4 = (s32[256]{0:T(256)S(1)}, s32[256]{0:T(256)}, u32[]{:S(2)}) copy-start(s32[256]{0:T(256)} %param.19) | copy-start | bytes 3076
  96.2 6.2 %copy-start.9 = (bf16[4,2,2,3,16,768]{5,4,3,2,1,0:T(8,128)(2,1)S(1)}, bf16[4,2,2,3,16,768]{5,4,3,2,1,0:T(8,128)(2,1)}, u32[]{:S(2)}) copy-start(bf16[4,2,2,3,16,768]{5,4,3,2,1,0:T(8,128)(2,1)} %get-tuple-element.38) | copy-start | bytes 3538948
  98.5 4.8 %copy-start.20 = (bf16[4,2,2,3,16,3072]{5,4,3,2,1,0:T(8,128)(2,1)S(1)}, bf16[4,2,2,3,16,3072]{5,4,3,2,1,0:T(8,128)(2,1)}, u32[]{:S(2)}) copy-start(bf16[4,2,2,3,16,3072]{5,4,3,2,1,0:T(8,128)(2,1)} %get-tuple-element.39) | copy-start | bytes 14155780
  102.3 2.5 %copy-start.2 = (bf16[256,768]{1,0:T(8,128)(2,1)}, bf16[256,768]{1,0:T(8,128)(2,1)S(1)}, u32[]{:S(2)}) copy-start(bf16[256,768]{1,0:T(8,128)(2,1)S(1)} %shard_map.305.refs_4_) | copy-start | bytes 1179652
  103.2 2.3 slice-start
  103.4 1.5 copy-start.15
  103.4 2.2 slice-start.1
  105.6 9.8 %copy-start.13 = (f32[256,3072]{1,0:T(8,128)}, f32[256,3072]{1,0:T(8,128)S(1)}, u32[]{:S(2)}) copy-start(f32[256,3072]{1,0:T(8,128)S(1)} %convolution_add_fusion) | copy-start | bytes 9437188
  115.4 2.4 %copy-start.16 = (bf16[256,3072]{1,0:T(8,128)(2,1)}, bf16[256,3072]{1,0:T(8,128)(2,1)S(1)}, u32[]{:S(2)}) copy-start(bf16[256,3072]{1,0:T(8,128)(2,1)S(1)} %get-tuple-element.69.refs_7_) | copy-start | bytes 4718596
  118.0 5.1 %slice-start.2 = ((s8[4718592]{0:T(1024)(128)(4,1)}), s8[4194304]{0:T(1024)(128)(4,1)S(1)}, s32[]{:S(2)}) async-start(s8[4718592]{0:T(1024)(128)(4,1)} %bitcast.114), calls=%async_computation.2 | async-start | bytes 8388608
  119.6 3.5 %slice-start.3 = ((s8[4718592]{0:T(1024)(128)(4,1)}), s8[524288]{0:T(1024)(128)(4,1)S(1)}, s32[]{:S(2)}) async-start(s8[4718592]{0:T(1024)(128)(4,1)} %bitcast.114), calls=%async_computation.3 | async-start | bytes 1048576
  123.1 2.2 copy-start.6
  125.3 11.0 %copy-start.18 = (bf16[4,2,2,3,16,768]{5,4,3,2,1,0:T(8,128)(2,1)S(1)}, bf16[4,2,2,3,16,768]{5,4,3,2,1,0:T(8,128)(2,1)}, u32[]{:S(2)}) copy-start(bf16[4,2,2,3,16,768]{5,4,3,2,1,0:T(8,128)(2,1)} %get-tuple-element.35) | copy-start | bytes 3538948
  126.6 0.8 copy-start.11
  127.4 9.5 %copy-start.8 = (bf16[4,2,2,3,16,768]{5,4,3,2,1,0:T(8,128)(2,1)S(1)}, bf16[4,2,2,3,16,768]{5,4,3,2,1,0:T(8,128)(2,1)}, u32[]{:S(2)}) copy-start(bf16[4,2,2,3,16,768]{5,4,3,2,1,0:T(8,128)(2,1)} %get-tuple-element.36) | copy-start | bytes 3538948
  136.3 2.4 copy-start.3
  136.3 2.5 %copy-start = (bf16[256,768]{1,0:T(8,128)(2,1)}, bf16[256,768]{1,0:T(8,128)(2,1)S(1)}, u32[]{:S(2)}) copy-start(bf16[256,768]{1,0:T(8,128)(2,1)S(1)} %get-tuple-element.41.refs_1_) | copy-start | bytes 1179652
  136.3 2.6 %copy-start.1 = (bf16[256,768]{1,0:T(8,128)(2,1)}, bf16[256,768]{1,0:T(8,128)(2,1)S(1)}, u32[]{:S(2)}) copy-start(bf16[256,768]{1,0:T(8,128)(2,1)S(1)} %get-tuple-element.43.refs_3_) | copy-start | bytes 1179652
  136.4 1.7 copy-start.17
  138.0 1.8 copy-start.12
  232.1 7.8 %copy-start.19 = (bf16[2,3,64,768]{3,2,1,0:T(8,128)(2,1)S(1)}, bf16[2,3,64,768]{3,2,1,0:T(8,128)(2,1)}, u32[]{:S(2)}) copy-start(bf16[2,3,64,768]{3,2,1,0:T(8,128)(2,1)} %get-tuple-element.50) | copy-start | bytes 1769476

commit v3 on v2

--- a/solution.py
+++ b/solution.py
@@ -208,8 +208,8 @@
 HALVES = 2
 THIRDS = 3
 MESH = pl.DeviceIdType.MESH
-GATHER_PIECE, GATHER_AHEAD, GATHER_LAGS = 16 * 768, 4, (2, 4)
-REDUCE_LAGS = (0, 2, 4, 6, 8, 10)
+GATHER_PIECE, GATHER_AHEAD, GATHER_LAGS = 16 * 768, 3, (2, 4)
+REDUCE_LAGS = (0, 2, 5, 7, 9, 12)
 
 
 def place():

time: 242 us -> 239 us (0.988)
  Pallas kernels: 180 us -> 177 us
where the time goes in v3:
time: 239 us
  Pallas kernels  177 us (74%)
  matrix products  24.1 us (10%)
  other arithmetic  23.1 us (10%)
  local copies, waits for them, and re-layouts  12.9 us (5%)
    pallas_call x1, Pallas kernels, reduce_all(): pl.pallas_call(kernel, out_shape=[jax.ShapeDtypeStruct((HALVES, THIRDS) +...  89.5 us
    pallas_call x1, Pallas kernels, gather_all(): pl.pallas_call(functools.partial(gather_kernel, pieces, count), out_shape...  76.9 us
    dot_general x6, matrix products, against(): lax.dot_general(left, right, (((1,), (1,)), ((), ())), preferred_element_...  15.7 us
    pallas_call x2, Pallas kernels, local_call(): pl.pallas_call(kernel, out_shape=[jax.ShapeDtypeStruct(arrays[0].shape, j...  10.8 us
    dot_general x6, matrix products, product(): return jnp.dot(left, right, preferred_element_type=jnp.float32)  8.34 us
    convert_element_type x5, other arithmetic, on_device(): s.reshape(shape).astype(jnp.float32)  7.77 us
    pad x8, local copies, waits for them, and re-layouts, on_device(): jnp.pad(params[i][None], ((0, 0), (0, lanes - width)))  5.34 us

profile of v3, /device:TPU:1, one launch (start us, length us, event | category | flops | bytes accessed | tf_op | source)
XLA Modules:
  0.0 238.5 jit_solution(4352346235046352137)
XLA Ops:
  0.7 0.7 pad.37
  1.4 0.7 pad.38
  2.0 0.7 pad.39
  2.7 0.7 pad.40
  3.4 0.7 pad.41
  4.0 0.7 pad.42
  4.7 0.7 pad.43
  5.3 0.7 pad.44
  6.0 0.7 concatenate.6
  6.7 0.7 compare_convert_fusion
  7.4 1.1 convert_reduce_fusion
  8.6 1.2 fusion.20
  9.8 0.6 pad.45
  10.4 0.8 copy.35.seg_col
  11.2 1.1 fusion.23.refs_9_
  12.4 76.9 %gather_parameters.1 = (bf16[4,2,2,3,16,128]{5,4,3,2,1,0:T(8,128)(2,1)}, bf16[4,2,2,3,16,768]{5,4,3,2,1,0:T(8,128)(2,1)}, bf16[4,2,2,3,16,768]{5,4,3,2,1,0:T(8,1...) custom-call(bf16[2,3,16,128]{3,2,1,0:T(8,128)(2,1)} %bitcast.107, ...), custom_call_target="tpu_custom_call" | custom-call | tf_op jit(solution)/shard_map/gather_parameters/pallas_call | solution.py:337
  89.3 0.8 slice_convert_fusion
  90.2 1.1 fusion.26
  91.3 0.1 reshape.326
  91.9 0.3 fusion.18.refs_0_
  92.2 1.9 fusion.10.values
  94.1 1.8 fusion.9.query
  95.9 0.5 convolution_convert_fusion.1.keys
  96.4 3.8 %shard_map.305.refs_4_ = bf16[256,768]{1,0:T(8,128)(2,1)S(1)} custom-call(s32[256,1]{1,0:T(8,128)S(1)} %copy.35.seg_col, s32[1,256]{1,0:T(1,128)S(1)} %bitcast.90, bf16[256,768]{1,0:T(8,128)(2,1)S(1)} %fusion.9.query, bf16[256,768]{1,0:T(8,128)(2,1)S(1)} %convolution_convert_fusion.1.keys, bf16[256,768]{1,0:T(8,128)(2,1)S(1)} %fusion.10.values), custom_call_target="tpu_custom_call" | custom-call | tf_op jit(solution)/shard_map/pallas_call | solution.py:102
  100.2 0.6 fusion.43
  100.8 0.2 multiply_reduce_fusion.2
  101.1 0.2 add_convert_fusion.1.refs_6_
  101.3 1.4 convolution_add_fusion
  102.8 0.6 slice-done
  103.4 0.1 slice-done.1
  103.5 9.8 %fusion.40 = (bf16[3072]{0:T(1024)(128)(2,1)S(1)}, bf16[256,3072]{1,0:T(8,128)(2,1)S(1)}, f32[256,3072]{1,0:T(8,128)}) fusion(f32[256,3072]{1,0:T(8,128)S(1)} %convolution_add_fusion, bf16[256,768]{1,0:T(8,128)(2,1)S(1)} %fusion.23.refs_9_, bf16[3072,768]{1,0:T(8,128)(2,1)S(1)} %bitcast.113), kind=kOutput, calls=%fused_computation.114 | convolution fusion | flops 1265366016 | bytes 12982272 | tf_op jit(solution)/shard_map/dot_general | solution.py:38
  113.3 2.4 %multiply_reduce_fusion = (bf16[768]{0:T(1024)(128)(2,1)S(1)}, f32[256]{0:T(256)S(1)}, bf16[768]{0:T(1024)(128)(2,1)S(1)}, f32[256,768]{1,0:T(8,128)}) fusion(f32[256,768]{1,0:T(8,128)S(1)} %get-tuple-element.83, f32[256]{0:T(256)S(1)} %fusion.35, f32[256]{0:T(256)S(1)} %broadcast_multiply_fusion, f32[768]{0:T(1024)S(1)} %reshape.323, ...), kind=kOutput, calls=%fused_computation.46 | convolution fusion | flops 1209530624 | bytes 7873536 | tf_op jit(solution)/shard_map/dot_general | solution.py:38
  115.8 0.1 convert_element_type.312
  115.9 1.6 fusion.42
  117.5 3.4 %multiply_convert_fusion.refs_8_ = bf16[256,3072]{1,0:T(8,128)(2,1)S(1)} fusion(f32[256,3072]{1,0:T(8,128)} %get-tuple-element.70, f32[256,3072]{1,0:T(8,128)} %copy-done.13), kind=kLoop, calls=%fused_computation.4 | loop fusion | flops 2359296 | bytes 7864320 | tf_op jit(solution)/shard_map/convert_element_type | solution.py:142
  121.0 2.1 fusion.8
  123.1 0.1 convert_element_type.314
  123.2 1.3 fusion.38.refs_5_
  124.5 0.7 copy-done.11
  125.3 1.9 convolution_convert_fusion.grad_mixed
  127.2 7.1 %shard_map.306 = (bf16[256,768]{1,0:T(8,128)(2,1)S(1)}, bf16[256,768]{1,0:T(8,128)(2,1)S(1)}, bf16[256,768]{1,0:T(8,128)(2,1)S(1)}) custom-call(s32[256,1]{1,0:T(8,128)S(1)} %copy.35.seg_col, s32[1,256]{1,0:T(1,128)S(1)} %bitcast.91, bf16[256,768]{1,0:T(8,128)(2,1)S(1)} %fusion.9.query, bf16[256,768]{1,0:T(8,128)(2,1)S(1)} %convolution_convert_fusion.1.keys, ...), custom_call_target="tpu_custom_call" | custom-call | tf_op jit(solution)/shard_map/pallas_call | solution.py:102
  134.3 0.5 fusion.44
  134.8 0.5 convolution_add_fusion.2
  135.3 0.6 copy-done.17
  135.9 0.6 fusion.39
  136.6 0.1 convert_element_type.308
  136.7 0.1 reduce_sum.182
  136.8 0.1 stack_reshape.4
  136.9 0.1 reduce_sum.183
  136.9 0.1 stack_reshape.5
  137.0 0.7 fusion.19
  137.7 0.1 convert_element_type.306
  137.8 1.4 fusion.22
  139.1 0.1 convert_element_type.316
  139.2 0.1 convert_element_type.310
  139.4 0.7 pad.47.clone
  140.1 89.5 %reduce_gradients.1 = (bf16[2,3,16,128]{3,2,1,0:T(8,128)(2,1)}, bf16[2,3,16,768]{3,2,1,0:T(8,128)(2,1)}, bf16[2,3,16,768]{3,2,1,0:T(8,128)(2,1)}, bf16[2,3,16,76...) custom-call(bf16[4,2,2,3,16,128]{5,4,3,2,1,0:T(8,128)(2,1)} %bitcast, ...), custom_call_target="tpu_custom_call" | custom-call | tf_op jit(solution)/shard_map/reduce_gradients/pallas_call | solution.py:531
  229.6 0.8 bitcast_convert_fusion.6
  230.4 0.6 slice_bitcast_fusion
  231.0 0.5 slice_bitcast_fusion.1
  231.6 1.8 bitcast_convert_fusion.4
  233.4 1.8 bitcast_convert_fusion.2
  235.2 2.2 bitcast_convert_fusion.1
  237.4 1.1 bitcast_convert_fusion
  (76 shorter events, 0.8 us)
Async XLA Ops:
  0.7 91.2 %copy-start.5 = (bf16[256,768]{1,0:T(8,128)(2,1)S(1)}, bf16[256,768]{1,0:T(8,128)(2,1)}, u32[]{:S(2)}) copy-start(bf16[256,768]{1,0:T(8,128)(2,1)} %param.18) | copy-start | bytes 1179652
  12.4 90.4 %copy-start.14 = (bf16[256,768]{1,0:T(8,128)(2,1)}, bf16[256,768]{1,0:T(8,128)(2,1)S(1)}, u32[]{:S(2)}) copy-start(bf16[256,768]{1,0:T(8,128)(2,1)S(1)} %fusion.23.refs_9_) | copy-start | bytes 1179652
  89.3 6.6 %copy-start.7 = (bf16[4,2,2,3,16,768]{5,4,3,2,1,0:T(8,128)(2,1)S(1)}, bf16[4,2,2,3,16,768]{5,4,3,2,1,0:T(8,128)(2,1)}, u32[]{:S(2)}) copy-start(bf16[4,2,2,3,16,768]{5,4,3,2,1,0:T(8,128)(2,1)} %get-tuple-element.36) | copy-start | bytes 3538948
  92.1 3.8 %copy-start.10 = (bf16[256,768]{1,0:T(8,128)(2,1)}, bf16[256,768]{1,0:T(8,128)(2,1)S(1)}, u32[]{:S(2)}) copy-start(bf16[256,768]{1,0:T(8,128)(2,1)S(1)} %fusion.18.refs_0_) | copy-start | bytes 1179652
  92.1 4.3 %copy-start.4 = (s32[256]{0:T(256)S(1)}, s32[256]{0:T(256)}, u32[]{:S(2)}) copy-start(s32[256]{0:T(256)} %param.19) | copy-start | bytes 3076
  94.1 6.2 %copy-start.9 = (bf16[4,2,2,3,16,768]{5,4,3,2,1,0:T(8,128)(2,1)S(1)}, bf16[4,2,2,3,16,768]{5,4,3,2,1,0:T(8,128)(2,1)}, u32[]{:S(2)}) copy-start(bf16[4,2,2,3,16,768]{5,4,3,2,1,0:T(8,128)(2,1)} %get-tuple-element.38) | copy-start | bytes 3538948
  96.4 4.8 %copy-start.20 = (bf16[4,2,2,3,16,3072]{5,4,3,2,1,0:T(8,128)(2,1)S(1)}, bf16[4,2,2,3,16,3072]{5,4,3,2,1,0:T(8,128)(2,1)}, u32[]{:S(2)}) copy-start(bf16[4,2,2,3,16,3072]{5,4,3,2,1,0:T(8,128)(2,1)} %get-tuple-element.39) | copy-start | bytes 14155780
  100.2 2.5 %copy-start.2 = (bf16[256,768]{1,0:T(8,128)(2,1)}, bf16[256,768]{1,0:T(8,128)(2,1)S(1)}, u32[]{:S(2)}) copy-start(bf16[256,768]{1,0:T(8,128)(2,1)S(1)} %shard_map.305.refs_4_) | copy-start | bytes 1179652
  101.1 2.3 slice-start
  101.3 1.5 copy-start.15
  101.3 2.2 slice-start.1
  103.5 9.8 %copy-start.13 = (f32[256,3072]{1,0:T(8,128)}, f32[256,3072]{1,0:T(8,128)S(1)}, u32[]{:S(2)}) copy-start(f32[256,3072]{1,0:T(8,128)S(1)} %convolution_add_fusion) | copy-start | bytes 9437188
  113.3 2.4 %copy-start.16 = (bf16[256,3072]{1,0:T(8,128)(2,1)}, bf16[256,3072]{1,0:T(8,128)(2,1)S(1)}, u32[]{:S(2)}) copy-start(bf16[256,3072]{1,0:T(8,128)(2,1)S(1)} %get-tuple-element.69.refs_7_) | copy-start | bytes 4718596
  115.9 5.1 %slice-start.2 = ((s8[4718592]{0:T(1024)(128)(4,1)}), s8[4194304]{0:T(1024)(128)(4,1)S(1)}, s32[]{:S(2)}) async-start(s8[4718592]{0:T(1024)(128)(4,1)} %bitcast.114), calls=%async_computation.2 | async-start | bytes 8388608
  117.5 3.5 %slice-start.3 = ((s8[4718592]{0:T(1024)(128)(4,1)}), s8[524288]{0:T(1024)(128)(4,1)S(1)}, s32[]{:S(2)}) async-start(s8[4718592]{0:T(1024)(128)(4,1)} %bitcast.114), calls=%async_computation.3 | async-start | bytes 1048576
  121.0 2.2 copy-start.6
  123.2 11.0 %copy-start.18 = (bf16[4,2,2,3,16,768]{5,4,3,2,1,0:T(8,128)(2,1)S(1)}, bf16[4,2,2,3,16,768]{5,4,3,2,1,0:T(8,128)(2,1)}, u32[]{:S(2)}) copy-start(bf16[4,2,2,3,16,768]{5,4,3,2,1,0:T(8,128)(2,1)} %get-tuple-element.35) | copy-start | bytes 3538948
  124.5 0.8 copy-start.11
  125.3 9.5 %copy-start.8 = (bf16[4,2,2,3,16,768]{5,4,3,2,1,0:T(8,128)(2,1)S(1)}, bf16[4,2,2,3,16,768]{5,4,3,2,1,0:T(8,128)(2,1)}, u32[]{:S(2)}) copy-start(bf16[4,2,2,3,16,768]{5,4,3,2,1,0:T(8,128)(2,1)} %get-tuple-element.36) | copy-start | bytes 3538948
  134.2 2.4 copy-start.3
  134.2 2.5 %copy-start = (bf16[256,768]{1,0:T(8,128)(2,1)}, bf16[256,768]{1,0:T(8,128)(2,1)S(1)}, u32[]{:S(2)}) copy-start(bf16[256,768]{1,0:T(8,128)(2,1)S(1)} %get-tuple-element.41.refs_1_) | copy-start | bytes 1179652
  134.2 2.6 %copy-start.1 = (bf16[256,768]{1,0:T(8,128)(2,1)}, bf16[256,768]{1,0:T(8,128)(2,1)S(1)}, u32[]{:S(2)}) copy-start(bf16[256,768]{1,0:T(8,128)(2,1)S(1)} %get-tuple-element.43.refs_3_) | copy-start | bytes 1179652
  134.3 1.7 copy-start.17
  135.9 1.8 copy-start.12
  229.6 7.8 %copy-start.19 = (bf16[2,3,64,768]{3,2,1,0:T(8,128)(2,1)S(1)}, bf16[2,3,64,768]{3,2,1,0:T(8,128)(2,1)}, u32[]{:S(2)}) copy-start(bf16[2,3,64,768]{3,2,1,0:T(8,128)(2,1)} %get-tuple-element.50) | copy-start | bytes 1769476
